TPU v7x, 768 devices: a whole 4x8x12 slice. The times are simulated.
768 devices in a mesh: mesh: 48 (over y, z_lo, core), event: 16 (over z_hi, x).
Axes of the slice: x: 4, y: 8, z: 12 (z_hi: 4, z_lo: 3; z = z_hi * 3 + z_lo), core: 2. Of those that a mesh axis runs over, the one named last changes fastest.
Arguments:
- forward_now: float32 [16, 3, 124848], P('event', None, 'mesh'), may hold values from -6 to 6
- forward_prev: float32 [16, 3, 124848], P('event', None, 'mesh'), may hold values from -6 to 6
- adjoint_now: float32 [16, 3, 124848], P('event', None, 'mesh'), may hold values from -6 to 6
- adjoint_prev: float32 [16, 3, 124848], P('event', None, 'mesh'), may hold values from -6 to 6
- connectivity: int32 [125, 1536], P(None, 'mesh'), may hold values from 0 to 2600, as said below
- lower_face: int32 [48, 289], P('mesh'), may hold values from 0 to 2600, as said below
- upper_face: int32 [48, 289], P('mesh'), may hold values from 0 to 2600, as said below
- bulk_modulus: float32 [125, 1536], P(None, 'mesh'), may hold values from 0.5 to 2
- shear_modulus: float32 [125, 1536], P(None, 'mesh'), may hold values from 0.3 to 1.2
- step_scale: float32 [124848], P('mesh'), may hold values from 0.0069 to 5.01, as said below
- receiver_points: int32 [6144], P('mesh'), may hold values from 0 to 2600
- adjoint_source: float32 [16, 2, 3, 6144], P('event', None, None, 'mesh'), may hold values from -18 to 18
Outputs:
- forward_next: float32 [16, 3, 124848], P('event', None, 'mesh')
- adjoint_next: float32 [16, 3, 124848], P('event', None, 'mesh')
- kernels: float32 [2, 125, 1536], P(None, None, ('mesh', 'event'))
Inputs may be any that keep to these rules, and one draw needn't show every extreme that they name: `connectivity`: each column lists local point numbers of its element's partition; every local point is used. A partition's elements come in 2 layers of 16: the first layer holds every point of the partition's lower_face, the last layer every point of its upper_face, and no other element touches those points. `lower_face`: distinct local point numbers, none in upper_face of the same partition; slot s of partition p's lower_face and slot s of partition p-1's upper_face are one shared point. `upper_face`: distinct local point numbers, none in lower_face of the same partition. `step_scale`: Positive.
All inputs are finite; a program needn't handle non-finite values.
Results may differ from a plain program's by a relative error of at most 0.0001.
Values sent between devices are 32-bit elements; how exact they have to be, the bound alone decides.
No kernel may reach another device: no remote copies, remote signals or barrier semaphores. Data moves between devices by JAX's collectives and lax.ppermute only.
A program may use at most 32 MiB of HBM per device.

v0:
```python
import math

import jax
import jax.numpy as jnp
import numpy as np
from jax import lax
from jax.sharding import PartitionSpec as P

STEPS = 2


kernel_weight = 0.02


def passed_along(value, axis, by):
    devices = lax.axis_size(axis)
    pairs = [(i, i + by) for i in range(devices) if 0 <= i + by < devices]
    return lax.ppermute(value, axis, pairs)


def derivative_table():
    root = math.sqrt(3.0 / 7.0)
    points = [-1.0, -root, 0.0, root, 1.0]
    legendre = [(35.0 * x**4 - 30.0 * x**2 + 3.0) / 8.0 for x in points]
    table = np.zeros((5, 5))
    for row in range(5):
        for column in range(5):
            if row != column:
                table[row, column] = (
                    legendre[row] / legendre[column] / (points[row] - points[column])
                )
    table[0, 0] = -2.5
    table[4, 4] = 2.5
    return table


def cube_weights():
    line = np.array([0.1, 49.0 / 90.0, 32.0 / 45.0, 49.0 / 90.0, 0.1])
    cube = line[:, None, None] * line[None, :, None] * line[None, None, :]
    return cube.reshape(125, 1)


def cube_tables():
    deriv = derivative_table()
    along_x = np.kron(np.eye(25), deriv)
    along_y = np.kron(np.eye(5), np.kron(deriv, np.eye(5)))
    along_z = np.kron(deriv, np.eye(25))
    return jnp.asarray(np.stack([along_x, along_y, along_z]), jnp.float32)


def element_terms(values, kappa, shear_mod, tables, quad):
    top = lax.Precision.HIGHEST
    grads = jnp.stack(
        [jnp.einsum("gh,fjhe->jfge", tables[i], values, precision=top) for i in range(3)]
    )
    strain = 0.5 * (grads + grads.transpose(1, 0, 2, 3, 4))
    dilation = strain[0, 0] + strain[1, 1] + strain[2, 2]
    unit = jnp.eye(3, dtype=jnp.float32)[:, :, None, None, None]
    deviator = strain - unit * (dilation / 3.0)
    stress = unit * (kappa * dilation) + 2.0 * shear_mod * deviator
    bulk = -kernel_weight * kappa * dilation[0] * dilation[1]
    shear = (
        -2.0
        * kernel_weight
        * shear_mod
        * jnp.sum(deviator[:, :, 0] * deviator[:, :, 1], axis=(0, 1))
    )
    weighted = quad * stress
    back = jnp.einsum("hg,jfhe->fjge", tables[0], weighted[0], precision=top)
    back = back + jnp.einsum("hg,jfhe->fjge", tables[1], weighted[1], precision=top)
    back = back + jnp.einsum("hg,jfhe->fjge", tables[2], weighted[2], precision=top)
    return (-back, bulk, shear)


def collect(waves, columns):
    count = columns.shape[1]
    flat = jnp.take(waves.reshape(6, waves.shape[2]), columns.reshape(-1), axis=1)
    return flat.reshape(2, 3, 125, count)


def deposit(forces, columns, element_force):
    points = forces.shape[2]
    flat = forces.reshape(6, points).at[:, columns.reshape(-1)].add(element_force.reshape(6, -1))
    return flat.reshape(2, 3, points)


def exchange_faces(upward, downward):
    below = passed_along(upward, "mesh", 1)
    above = passed_along(downward, "mesh", -1)
    return (below, above)


def shards(
    forward_now,
    forward_prev,
    adjoint_now,
    adjoint_prev,
    connectivity,
    lower_face,
    upper_face,
    bulk_modulus,
    shear_modulus,
    step_scale,
    receiver_points,
    adjoint_source,
):
    tables = cube_tables()
    quad = jnp.asarray(cube_weights(), jnp.float32)
    waves = jnp.concatenate([forward_now, adjoint_now], 0)
    before = jnp.concatenate([forward_prev, adjoint_prev], 0)
    lower = lower_face[0]
    upper = upper_face[0]
    sources = adjoint_source[0]
    count = connectivity.shape[1]
    points = waves.shape[2]
    totals = jnp.zeros((2, 125, count), jnp.float32)
    for step in range(STEPS):
        injected = jnp.zeros((3, points), jnp.float32).at[:, receiver_points].add(sources[step])
        forces = jnp.stack([jnp.zeros_like(injected), injected])
        element_force, bulk, shear = element_terms(
            collect(waves, connectivity), bulk_modulus, shear_modulus, tables, quad
        )
        forces = deposit(forces, connectivity, element_force)
        below, above = exchange_faces(forces[:, :, upper], forces[:, :, lower])
        forces = forces.at[:, :, lower].add(below).at[:, :, upper].add(above)
        following = 2.0 * waves - before + step_scale * forces
        before = waves
        waves = following
        totals = totals + jnp.stack([bulk, shear])
    owned = lax.psum_scatter(totals, "event", scatter_dimension=2, tiled=True)
    return (waves[0:1], waves[1:2], owned)


def solution(mesh):
    placed = (
        P("event", None, "mesh"),
        P("event", None, "mesh"),
        P("event", None, "mesh"),
        P("event", None, "mesh"),
        P(None, "mesh"),
        P("mesh", None),
        P("mesh", None),
        P(None, "mesh"),
        P(None, "mesh"),
        P("mesh"),
        P("mesh"),
        P("event", None, None, "mesh"),
    )
    return jax.shard_map(
        shards,
        mesh=mesh,
        in_specs=placed,
        out_specs=(
            P("event", None, "mesh"),
            P("event", None, "mesh"),
            P(None, None, ("mesh", "event")),
        ),
        check_vma=False,
    )
```

profile of v0, /device:TPU:32, one launch (start us, length us, event | category | flops | bytes accessed | tf_op | source)
XLA Modules:
  0.0 325.3 jit_solution(2866589842878115658)
XLA Ops:
  3.7 14.2 %gather_fusion.4 = f32[4000,6]{1,0:T(8,128)} fusion(f32[6,2601]{0,1:T(8,128)S(1)} %copy.212, s32[4096]{0:T(1024)S(1)} %pad_clamp_fusion), kind=kCustom, calls=%fused_computation.clone | custom fusion | bytes 208000 | tf_op jit(solution)/shard_map/jit(_take)/gather | solution.py:77
  17.8 3.6 %select_bitcast_fusion.1 = f32[6,4000]{0,1:T(8,128)S(1)} fusion(f32[4000,6]{1,0:T(8,128)} %gather_fusion.4, pred[4000]{0:T(1024)(128)(4,1)S(1)} %compare_and_fusion), kind=kLoop, calls=%fused_computation.15 | loop fusion | flops 24000 | bytes 196000 | tf_op jit(solution)/shard_map/jit(_take)/select_n | solution.py:77
  24.7 0.8 add_multiply_fusion.1
  29.3 1.6 scatter_custom_fusion
  31.0 1.0 copy.274
  32.9 1.5 copy.225
  35.1 22.9 %scatter_fusion = f32[6,2601]{0,1:T(8,128)} fusion(f32[6,2601]{0,1:T(8,128)} %copy.225, s32[4000]{0:T(1024)S(1)} %bitcast.181, f32[4000,6]{1,0:T(8,128)S(1)} %copy.226), kind=kCustom, calls=%fused_computation.7 | custom fusion | flops 24000 | bytes 304000 | tf_op jit(solution)/shard_map/scatter-add | solution.py:83
  58.0 2.9 reshape.301
  61.0 2.4 gather_fusion
  63.4 1.9 collective-permute-start
  65.4 2.4 gather_fusion.1
  67.8 6.8 %collective-permute-start.1 = (f32[2,3,289]{1,0,2:T(2,128)}, f32[2,3,289]{1,0,2:T(2,128)}, u32[]{:S(2)}, u32[]{:S(2)}) collective-permute-start(f32[2,3,289]{1,0,2:T(2,128)} %bitcast.186), channel_id=1, source_target_pairs={{16,0},{32,16},{48,32},{64,48},{80,64},{96,80},{112,96},{128,112},... | collective-permute-start | bytes 20816 | tf_op jit(solution)/shard_map/ppermute | solution.py:18
  74.8 2.2 scatter_custom_fusion.4
  77.1 1.7 copy.275
  79.0 1.5 copy.247
  80.5 1.3 dynamic-slice
  82.4 19.6 %scatter_fusion.1 = f32[2,3,2601]{1,0,2:T(2,128)S(1)} fusion(f32[2,3,2601]{1,0,2:T(2,128)S(1)} %reshape.301, s32[289]{0:T(512)S(1)} %fusion.33, f32[289,2,3]{2,1,0:T(2,128)} %bitcast.29), kind=kCustom, calls=%fused_computation.8 | custom fusion | flops 1734 | bytes 21964 | tf_op jit(solution)/shard_map/scatter-add | solution.py:125
  102.1 19.6 %scatter_fusion.2 = f32[2,3,2601]{1,0,2:T(2,128)S(1)} fusion(f32[2,3,2601]{1,0,2:T(2,128)S(1)} %scatter_fusion.1, s32[289]{0:T(512)S(1)} %fusion.34, f32[289,2,3]{2,1,0:T(2,128)} %bitcast.31), kind=kCustom, calls=%fused_computation.9 | custom fusion | flops 1734 | bytes 21964 | tf_op jit(solution)/shard_map/scatter-add | solution.py:125
  121.7 2.5 copy.231
  124.9 14.1 %gather_fusion.5 = f32[4000,6]{1,0:T(8,128)} fusion(f32[6,2601]{0,1:T(8,128)S(1)} %copy.235, s32[4096]{0:T(1024)S(1)} %copy-done.11), kind=kCustom, calls=%fused_computation.1.clone | custom fusion | bytes 208000 | tf_op jit(solution)/shard_map/jit(_take)/gather | solution.py:77
  139.0 3.6 %select_bitcast_fusion = f32[6,4000]{0,1:T(8,128)S(1)} fusion(f32[4000,6]{1,0:T(8,128)} %gather_fusion.5, pred[4000]{0:T(1024)(128)(4,1)S(1)} %compare_and_fusion), kind=kLoop, calls=%fused_computation.14 | loop fusion | flops 24000 | bytes 196000 | tf_op jit(solution)/shard_map/jit(_take)/select_n | solution.py:77
  147.9 22.9 %scatter_fusion.3 = f32[6,2601]{0,1:T(8,128)} fusion(f32[6,2601]{0,1:T(8,128)} %copy.247, s32[4000]{0:T(1024)S(1)} %bitcast.182, f32[4000,6]{1,0:T(8,128)S(1)} %copy.248), kind=kCustom, calls=%fused_computation.11 | custom fusion | flops 24000 | bytes 304000 | tf_op jit(solution)/shard_map/scatter-add | solution.py:83
  170.8 2.9 reshape.302
  173.7 2.4 gather_fusion.2
  176.1 2.4 gather_fusion.3
  178.6 98.6 %all-reduce.2 = f32[2,125,32]{1,2,0:T(8,128)S(1)} all-reduce(f32[2,125,32]{1,2,0:T(8,128)S(1)} %maximum_add_fusion), channel_id=2, replica_groups=mesh['mesh'=48,'event'=16] {'event'}, use_global_device_ids=true, to_apply=%region_10.12.clone | all-reduce | flops 8000 | bytes 64000
  277.3 1.9 collective-permute-start.2
  279.2 6.7 %collective-permute-start.3 = (f32[2,3,289]{1,0,2:T(2,128)}, f32[2,3,289]{1,0,2:T(2,128)S(1)}, u32[]{:S(2)}, u32[]{:S(2)}) collective-permute-start(f32[2,3,289]{1,0,2:T(2,128)} %bitcast.187), channel_id=1, source_target_pairs={{16,0},{32,16},{48,32},{64,48},{80,64},{96,80},{112,96},{128,112},... | collective-permute-start | bytes 20816 | tf_op jit(solution)/shard_map/ppermute | solution.py:18
  286.4 3.8 %collective-permute-done.2 = f32[2,3,289]{1,0,2:T(2,128)S(1)} collective-permute-done((f32[2,3,289]{1,0,2:T(2,128)}, f32[2,3,289]{1,0,2:T(2,128)S(1)}, u32[]{:S(2)}, u32[]{:S(2)}) %collective-permute-start.2) | collective-permute-done | bytes 6968 | tf_op jit(solution)/shard_map/ppermute | solution.py:18
  290.9 19.6 %scatter_fusion.4 = f32[2,3,2601]{1,0,2:T(2,128)S(1)} fusion(f32[2,3,2601]{1,0,2:T(2,128)S(1)} %reshape.302, s32[289]{0:T(512)S(1)} %fusion.33, f32[289,2,3]{2,1,0:T(2,128)} %bitcast.184), kind=kCustom, calls=%fused_computation.12 | custom fusion | flops 1734 | bytes 21964 | tf_op jit(solution)/shard_map/scatter-add | solution.py:125
  310.5 11.4 %scatter_fusion.5 = f32[2,3,2601]{1,0,2:T(2,128)S(1)} fusion(f32[2,3,2601]{1,0,2:T(2,128)S(1)} %scatter_fusion.4, s32[289]{0:T(512)S(1)} %fusion.34, f32[289,2,3]{2,1,0:T(2,128)S(1)} %bitcast.183), kind=kCustom, calls=%fused_computation.13 | custom fusion | flops 1734 | bytes 21964 | tf_op jit(solution)/shard_map/scatter-add | solution.py:125
  321.9 2.5 copy.253
  (134 shorter events, 19.6 us)
Async XLA Ops:
  2.3 1.4 copy-start.10
  21.4 0.8 copy-start.1
  21.4 1.6 copy-start.2
  21.4 2.4 copy-start.3
  22.1 2.6 copy-start.12
  22.1 2.6 copy-start.19
  22.1 2.6 copy-start.24
  24.7 1.4 copy-start.8
  25.6 1.8 copy-start.23
  25.9 2.9 copy-start.29
  58.0 2.9 copy-start.26
  58.0 7.3 %copy-start.27 = (s32[1,289]{1,0:T(1,128)S(1)}, s32[1,289]{1,0:T(1,128)}, u32[]{:S(2)}) copy-start(s32[1,289]{1,0:T(1,128)} %param.21) | copy-start | bytes 3472
  58.0 16.6 %copy-start = (f32[3,3,2,125,32]{3,4,1,2,0:T(8,128)S(1)}, f32[3,3,2,125,32]{3,4,1,2,0:T(8,128)}, u32[]{:S(2)}) copy-start(f32[3,3,2,125,32]{3,4,1,2,0:T(8,128)} %get-tuple-element.21) | copy-start | bytes 864004
  58.0 16.7 %copy-start.22 = (f32[128,3]{0,1:T(4,128)S(1)}, f32[128,3]{0,1:T(4,128)}, u32[]{:S(2)}) copy-start(f32[128,3]{0,1:T(4,128)} %get-tuple-element.38) | copy-start | bytes 4612
  63.4 19.0 %collective-permute-start = (f32[2,3,289]{1,0,2:T(2,128)}, f32[2,3,289]{1,0,2:T(2,128)}, u32[]{:S(2)}, u32[]{:S(2)}) collective-permute-start(f32[2,3,289]{1,0,2:T(2,128)} %bitcast.185), channel_id=1, source_target_pairs={{0,16},{16,32},{32,48},{48,64},{64,80},{80,96},{96,112},{112,128},... | collective-permute-start | bytes 20816 | tf_op jit(solution)/shard_map/ppermute | solution.py:18
  67.8 34.2 %collective-permute-start.1 = (f32[2,3,289]{1,0,2:T(2,128)}, f32[2,3,289]{1,0,2:T(2,128)}, u32[]{:S(2)}, u32[]{:S(2)}) collective-permute-start(f32[2,3,289]{1,0,2:T(2,128)} %bitcast.186), channel_id=1, source_target_pairs={{16,0},{32,16},{48,32},{64,48},{80,64},{96,80},{112,96},{128,112},... | collective-permute-start | bytes 20816 | tf_op jit(solution)/shard_map/ppermute | solution.py:18
  78.9 45.3 %copy-start.5 = (f32[1,3,2601]{2,0,1:T(1,128)S(1)}, f32[1,3,2601]{2,0,1:T(1,128)}, u32[]{:S(2)}) copy-start(f32[1,3,2601]{2,0,1:T(1,128)} %param.18) | copy-start | bytes 93640
  78.9 45.3 %copy-start.6 = (f32[1,3,2601]{2,0,1:T(1,128)S(1)}, f32[1,3,2601]{2,0,1:T(1,128)}, u32[]{:S(2)}) copy-start(f32[1,3,2601]{2,0,1:T(1,128)} %param.16) | copy-start | bytes 93640
  78.9 45.3 %copy-start.14 = (f32[1,3,2601]{2,0,1:T(1,128)S(1)}, f32[1,3,2601]{2,0,1:T(1,128)}, u32[]{:S(2)}) copy-start(f32[1,3,2601]{2,0,1:T(1,128)} %param.19) | copy-start | bytes 93640
  78.9 45.3 %copy-start.15 = (f32[1,3,2601]{2,0,1:T(1,128)S(1)}, f32[1,3,2601]{2,0,1:T(1,128)}, u32[]{:S(2)}) copy-start(f32[1,3,2601]{2,0,1:T(1,128)} %param.17) | copy-start | bytes 93640
  78.9 45.3 %copy-start.21 = (f32[2601]{0:T(1024)S(1)}, f32[2601]{0:T(1024)}, u32[]{:S(2)}) copy-start(f32[2601]{0:T(1024)} %param.25) | copy-start | bytes 31216
  121.7 3.2 copy-start.11
  142.6 1.6 copy-start.17
  142.6 2.4 copy-start.16
  143.3 2.6 copy-start.13
  143.3 2.6 copy-start.9
  143.3 2.6 copy-start.25
  144.2 1.9 copy-start.4
  170.8 7.8 %copy-start.20 = (f32[125,32]{0,1:T(8,128)S(1)}, f32[125,32]{0,1:T(8,128)}, u32[]{:S(2)}) copy-start(f32[125,32]{0,1:T(8,128)} %param.24) | copy-start | bytes 48004
  173.7 150.8 %copy-start.7 = (f32[1,3,2601]{2,0,1:T(1,128)S(1)}, f32[1,3,2601]{2,0,1:T(1,128)}, u32[]{:S(2)}) copy-start(f32[1,3,2601]{2,0,1:T(1,128)} %param.16) | copy-start | bytes 93640
  277.3 12.9 %collective-permute-start.2 = (f32[2,3,289]{1,0,2:T(2,128)}, f32[2,3,289]{1,0,2:T(2,128)S(1)}, u32[]{:S(2)}, u32[]{:S(2)}) collective-permute-start(f32[2,3,289]{1,0,2:T(2,128)} %bitcast.188), channel_id=1, source_target_pairs={{0,16},{16,32},{32,48},{48,64},{64,80},{80,96},{96,112},{112,128},... | collective-permute-start | bytes 20816 | tf_op jit(solution)/shard_map/ppermute | solution.py:18
  279.2 31.3 %collective-permute-start.3 = (f32[2,3,289]{1,0,2:T(2,128)}, f32[2,3,289]{1,0,2:T(2,128)S(1)}, u32[]{:S(2)}, u32[]{:S(2)}) collective-permute-start(f32[2,3,289]{1,0,2:T(2,128)} %bitcast.187), channel_id=1, source_target_pairs={{16,0},{32,16},{48,32},{64,48},{80,64},{96,80},{112,96},{128,112},... | collective-permute-start | bytes 20816 | tf_op jit(solution)/shard_map/ppermute | solution.py:18
  (2 other events, 1.5 us)
where the time goes:
time: 331 us; the launch traced here: 325 us
  other arithmetic  131 us (40%)
  blocking collectives  98.6 us (30%)
  local copies, waits for them, and re-layouts  66.6 us (20%)
  starting transfers between devices  17.3 us (5%)
  matrix products  6 us (2%)
  waiting for transfers between devices  3.77 us (1%)
    unnamed x1, blocking collectives  98.6 us
    scatter-add x4, other arithmetic, shards(): forces = forces.at[:, :, lower].add(below).at[:, :, upper].add(above)  70.2 us
    scatter-add x2, other arithmetic, deposit(): forces.reshape(6, points).at[:, columns.reshape(-1)]  45.9 us
    gather x2, local copies, waits for them, and re-layouts, collect(): jnp.take(waves.reshape(6, waves.shape[2]), columns.reshape(-1), axis=1)  28.3 us
    ppermute x4, starting transfers between devices, passed_along(): return lax.ppermute(value, axis, pairs)  17.3 us
    gather x4, local copies, waits for them, and re-layouts, shards(): below, above = exchange_faces(forces[:, :, upper], forces[:, :, lower])  9.73 us
    select_n x3, other arithmetic, collect(): jnp.take(waves.reshape(6, waves.shape[2]), columns.reshape(-1), axis=1)  7.13 us
  transfers between devices with their start and end apart: 4, of which 1 were waited for; matrix products, arithmetic and copies ran while one was open for 15% of the time, Pallas kernels for 0%

commit v1 on v0

v1 whole, which is shorter than its diff:
```python
import functools
import math

import jax
import jax.numpy as jnp
import numpy as np
from jax import lax
from jax.experimental import pallas as pl
from jax.experimental.pallas import tpu as pltpu
from jax.sharding import PartitionSpec as P

F32 = jnp.float32
BF16 = jnp.bfloat16
EVENTS = 16
FIELDS = 6
ELEMS = 32
CUBE = 125
POINTS = 2601
FACE = 289
LANES = 128
WIDE = 256
FINE = 21
COARSE = 11
PADDED = COARSE * WIDE
RECEIVER_ROW = 32
FACE_ROW = 40
KERNEL_WEIGHT = 0.02

VMEM = pl.BlockSpec(memory_space=pltpu.VMEM)
MIB = 1024 * 1024


def derivative_table():
    root = math.sqrt(3.0 / 7.0)
    points = [-1.0, -root, 0.0, root, 1.0]
    legendre = [(35.0 * x**4 - 30.0 * x**2 + 3.0) / 8.0 for x in points]
    table = np.zeros((5, 5))
    for row in range(5):
        for column in range(5):
            if row != column:
                table[row, column] = (
                    legendre[row] / legendre[column] / (points[row] - points[column])
                )
    table[0, 0] = -2.5
    table[4, 4] = 2.5
    return table


def cube_tables():
    deriv = derivative_table().astype(np.float32).astype(np.float64)
    line = np.array([0.1, 49.0 / 90.0, 32.0 / 45.0, 49.0 / 90.0, 0.1])
    cube = (line[:, None, None] * line[None, :, None] * line[None, None, :]).reshape(CUBE)
    cube = cube.astype(np.float32).astype(np.float64)
    along = [
        np.kron(np.eye(25), deriv),
        np.kron(np.eye(5), np.kron(deriv, np.eye(5))),
        np.kron(deriv, np.eye(25)),
    ]
    ahead = np.zeros((3 * LANES, LANES))
    back = np.zeros((3 * LANES, LANES))
    for i in range(3):
        ahead[i * LANES : i * LANES + CUBE, :CUBE] = along[i]
        back[i * LANES : i * LANES + CUBE, :CUBE] = -cube[:, None] * along[i]
    return (jnp.asarray(ahead, F32), jnp.asarray(back, F32))


def split(value):
    high = value.astype(BF16)
    return (high, (value - high.astype(F32)).astype(BF16))


def product(value, table, side):
    high, low = split(value)
    table_high, table_low = split(table)

    def dot(a, b):
        return lax.dot_general(a, b, (((1,), (side,)), ((), ())), preferred_element_type=F32)

    return dot(high, table_high) + (dot(low, table_high) + dot(high, table_low))


def pick(row, lanes):
    return jnp.take_along_axis(row, lanes, axis=1, mode="promise_in_bounds")


def gather_elements(wave_ref, index):
    fine = index >> 7
    lane = index & 127
    found = [jnp.zeros((ELEMS, LANES), F32) for _ in range(FIELDS)]
    for c in range(FINE):
        hit = fine == c
        for r in range(FIELDS):
            row = wave_ref[r : r + 1, c * LANES : (c + 1) * LANES]
            got = pick(jnp.broadcast_to(row, (ELEMS, LANES)), lane)
            found[r] = jnp.where(hit, got, found[r])
    return found


def gather_faces(forces, index_ref, inner_ref, outer_ref):
    for tile in range(6):
        index = jnp.broadcast_to(index_ref[FACE_ROW + tile : FACE_ROW + tile + 1, :], (8, LANES))
        fine = index >> 7
        lane = index & 127
        found = jnp.zeros((8, LANES), F32)
        for c in range(FINE):
            block = forces[c // 2][:, (c % 2) * LANES : (c % 2 + 1) * LANES]
            found = jnp.where(fine == c, pick(block, lane), found)
        if tile < 3:
            inner_ref[tile * 8 : tile * 8 + 8, :] = found
        else:
            outer_ref[(tile - 3) * 8 : (tile - 3) * 8 + 8, :] = found


def scatter(tiles, rows, index_ref, left_ref, right_ref):
    step = lax.broadcasted_iota(jnp.int32, (16, LANES), 0)
    for t, (tile, row) in enumerate(zip(tiles, rows)):
        lanes = slice(t * LANES, (t + 1) * LANES)
        index = jnp.broadcast_to(index_ref[row : row + 1, :], (16, LANES))
        coarse = (index >> 8).astype(F32).astype(BF16)
        offset = ((index & 255) - step).astype(F32).astype(BF16)
        high = tile.astype(BF16).astype(F32)
        both = jnp.concatenate([high, tile - high], 0).astype(BF16)
        for c in range(COARSE):
            left_ref[c * 16 : (c + 1) * 16, lanes] = jnp.where(coarse == c, both, jnp.zeros_like(both))
        for c in range(16):
            right_ref[c * 16 : (c + 1) * 16, lanes] = jnp.where(
                offset == c * 16, jnp.ones_like(both), jnp.zeros_like(both)
            )
    width = len(rows) * LANES
    total = lax.dot_general(
        left_ref[:, :width],
        right_ref[:, :width],
        (((1,), (1,)), ((), ())),
        preferred_element_type=F32,
    )
    return [total[c * 16 : c * 16 + 8] + total[c * 16 + 8 : c * 16 + 16] for c in range(COARSE)]


def element_terms(fields, kappa, shear_mod, ahead, back):
    grads = product(jnp.concatenate(fields, 0), ahead[...], 1)

    def grad(f, i, j):
        r = (3 * f + j) * ELEMS
        return grads[r : r + ELEMS, i * LANES : (i + 1) * LANES]

    columns = []
    dilations = []
    deviators = []
    for f in range(2):
        normal = [grad(f, i, i) for i in range(3)]
        dilation = normal[0] + normal[1] + normal[2]
        deviator = [n - dilation * (1.0 / 3.0) for n in normal]
        shear = {
            (i, j): 0.5 * (grad(f, i, j) + grad(f, j, i)) for i, j in ((0, 1), (0, 2), (1, 2))
        }
        pressure = kappa * dilation
        twice = 2.0 * shear_mod
        for j in range(3):
            stress = [
                pressure + twice * deviator[j] if i == j else twice * shear[min(i, j), max(i, j)]
                for i in range(3)
            ]
            columns.append(jnp.concatenate(stress, 1))
        dilations.append(dilation)
        deviators.append((deviator, shear))
    bulk = -KERNEL_WEIGHT * kappa * dilations[0] * dilations[1]
    (normal0, shear0), (normal1, shear1) = deviators
    inner = normal0[0] * normal1[0] + normal0[1] * normal1[1] + normal0[2] * normal1[2]
    cross = sum(shear0[key] * shear1[key] for key in shear0)
    shear = -2.0 * KERNEL_WEIGHT * shear_mod * (inner + 2.0 * cross)
    forces = product(jnp.concatenate(columns, 0), back[...], 0)
    return (forces, bulk, shear)


def local_step(wave_ref, moduli_ref, index_ref, source_ref, step, tables, tile_ref, left_ref, right_ref):
    kappa = moduli_ref[0:ELEMS, :]
    shear_mod = moduli_ref[ELEMS : 2 * ELEMS, :]
    fields = gather_elements(wave_ref, index_ref[0:ELEMS, :])
    element_force, bulk, shear = element_terms(fields, kappa, shear_mod, *tables)
    tile_ref[...] = jnp.zeros_like(tile_ref)
    for r in range(FIELDS):
        tile_ref[pl.ds(r, ELEMS, stride=8), :] = element_force[r * ELEMS : (r + 1) * ELEMS]
    for j in range(3):
        row = RECEIVER_ROW * 8 + 3 + j
        tile_ref[row : row + 1, :] = source_ref[j, step : step + 1, :]
    count = RECEIVER_ROW + 2
    tiles = [tile_ref[8 * t : 8 * t + 8, :] for t in range(count)]
    forces = scatter(tiles, list(range(count)), index_ref, left_ref, right_ref)
    return (forces, bulk, shear)


def add_faces(inner_ref, outer_ref, index_ref, left_ref, right_ref):
    tiles = [ref[8 * t : 8 * t + 8, :] for ref in (inner_ref, outer_ref) for t in range(3)]
    return scatter(tiles, [FACE_ROW + t for t in range(6)], index_ref, left_ref, right_ref)


def block(c):
    return slice(c * WIDE, (c + 1) * WIDE)


def first_kernel(*refs):
    inputs, refs = refs[:14], refs[14:]
    wave, force, index, moduli, to_inner, to_outer, totals = refs[:7]
    kept, refs = refs[7:13], refs[13:]
    source, tables = kept[0], kept[4:]
    arrived, (tiles, left, right, sems) = refs[:8], refs[8:]
    copies = [
        pltpu.make_async_copy(source, target, sems.at[i])
        for i, (source, target) in enumerate(zip(inputs, arrived + kept))
    ]
    for copy in copies:
        copy.start()
    forward, adjoint, connectivity, receivers, lower, upper, bulk_modulus, shear_modulus = arrived
    for ref in (wave, moduli):
        ref[...] = jnp.zeros_like(ref)
    index[0:FACE_ROW, :] = jnp.zeros((FACE_ROW, LANES), jnp.int32)
    index[FACE_ROW:, :] = jnp.full((8, LANES), -1, jnp.int32)
    for copy in copies[:9] + copies[12:]:
        copy.wait()
    for j in range(3):
        wave[j : j + 1, 0:POINTS] = forward[j]
        wave[3 + j : 4 + j, 0:POINTS] = adjoint[j]
    index[0:ELEMS, 0:CUBE] = connectivity[...]
    index[RECEIVER_ROW : RECEIVER_ROW + 1, :] = receivers[...]
    even = lax.rem(lax.axis_index("mesh"), 2) == 0
    inner = jnp.where(even, upper[...], lower[...])
    outer = jnp.where(even, lower[...], upper[...])
    for t in range(3):
        size = min(LANES, FACE - t * LANES)
        part = slice(t * LANES, t * LANES + size)
        index[FACE_ROW + t : FACE_ROW + t + 1, 0:size] = inner[:, part]
        index[FACE_ROW + 3 + t : FACE_ROW + 4 + t, 0:size] = outer[:, part]
    moduli[0:ELEMS, 0:CUBE] = bulk_modulus[...]
    moduli[ELEMS : 2 * ELEMS, 0:CUBE] = shear_modulus[...]
    forces, bulk, shear = local_step(wave, moduli, index, source, 0, tables, tiles, left, right)
    gather_faces(forces, index, to_inner, to_outer)
    for c in range(COARSE):
        force[:, block(c)] = forces[c]
    totals[0:ELEMS, :] = bulk
    totals[ELEMS : 2 * ELEMS, :] = shear
    for copy in copies[9:12]:
        copy.wait()


def second_kernel(
    from_inner,
    from_outer,
    wave,
    force,
    forward_prev,
    adjoint_prev,
    step_scale,
    index,
    moduli,
    source,
    earlier,
    ahead,
    back,
    following,
    scale,
    to_inner,
    to_outer,
    terms,
    now,
    sums,
    tiles,
    left,
    right,
):
    scale[...] = jnp.zeros_like(scale)
    following[...] = jnp.zeros_like(following)
    scale[0:1, 0:POINTS] = step_scale[...].reshape(1, POINTS)
    for j in range(3):
        following[j : j + 1, 0:POINTS] = forward_prev[j]
        following[3 + j : 4 + j, 0:POINTS] = adjoint_prev[j]
    added = add_faces(from_inner, from_outer, index, left, right)
    for c in range(COARSE):
        now[:, block(c)] = (
            2.0 * wave[:, block(c)]
            - following[:, block(c)]
            + scale[0:1, block(c)] * (force[:, block(c)] + added[c])
        )
    tables = (ahead, back)
    forces, bulk, shear = local_step(now, moduli, index, source, 1, tables, tiles, left, right)
    gather_faces(forces, index, to_inner, to_outer)
    for c in range(COARSE):
        following[:, block(c)] = (
            2.0 * now[:, block(c)] - wave[:, block(c)] + scale[0:1, block(c)] * forces[c]
        )
    sums[0:ELEMS, :] = earlier[0:ELEMS, :] + bulk
    sums[ELEMS : 2 * ELEMS, :] = earlier[ELEMS : 2 * ELEMS, :] + shear
    for which in range(2):
        for e in range(2):
            terms[:, 2 * which + e, :] = sums[pl.ds(which * ELEMS + e, EVENTS, stride=2), :]


def third_kernel(from_inner, from_outer, local, scale, index, terms, forward, adjoint, kernels, now, left, right):
    added = add_faces(from_inner, from_outer, index, left, right)
    for c in range(COARSE):
        now[:, block(c)] = local[:, block(c)] + scale[0:1, block(c)] * added[c]
    for j in range(3):
        forward[j] = now[j : j + 1, 0:POINTS]
        adjoint[j] = now[3 + j : 4 + j, 0:POINTS]
    owned = jnp.sum(terms[...], axis=0)
    for which in range(2):
        kernels[which] = owned[2 * which : 2 * which + 2, 0:CUBE]


def call(kernel, outs, scratch, args, place=VMEM):
    return pl.pallas_call(
        kernel,
        out_shape=[jax.ShapeDtypeStruct(shape, dtype) for shape, dtype in outs],
        in_specs=[place] * len(args),
        out_specs=[VMEM] * len(outs),
        scratch_shapes=scratch,
        compiler_params=pltpu.CompilerParams(vmem_limit_bytes=16 * MIB),
    )(*args)


def swap_faces(to_inner, to_outer):
    count = lax.axis_size("mesh")
    inner = [(i, i ^ 1) for i in range(count)]
    outer = [(i, i + 1 if i % 2 else i - 1) for i in range(1, count - 1)]
    return (lax.ppermute(to_inner, "mesh", inner), lax.ppermute(to_outer, "mesh", outer))


def shards(
    forward_now,
    forward_prev,
    adjoint_now,
    adjoint_prev,
    connectivity,
    lower_face,
    upper_face,
    bulk_modulus,
    shear_modulus,
    step_scale,
    receiver_points,
    adjoint_source,
):
    def rows(field):
        return field.transpose(1, 0, 2)

    tables = cube_tables()
    source = adjoint_source[0].transpose(1, 0, 2)
    padded = ((8, PADDED), F32)
    face = ((24, LANES), F32)
    pair = ((2 * ELEMS, LANES), F32)
    wide = (RECEIVER_ROW + 2) * LANES
    work = [
        pltpu.VMEM(((RECEIVER_ROW + 2) * 8, LANES), F32),
        pltpu.VMEM((COARSE * 16, wide), BF16),
        pltpu.VMEM((WIDE, wide), BF16),
    ]
    inputs = [
        rows(forward_now),
        rows(adjoint_now),
        connectivity.T,
        receiver_points.reshape(1, LANES),
        lower_face,
        upper_face,
        bulk_modulus.T,
        shear_modulus.T,
        source,
        rows(forward_prev),
        rows(adjoint_prev),
        step_scale,
        *tables,
    ]
    inputs = [pltpu.with_memory_space_constraint(value, pltpu.HBM) for value in inputs]
    wave, force, index, moduli, to_inner, to_outer, earlier, *kept = call(
        first_kernel,
        [padded, padded, ((48, LANES), jnp.int32), pair, face, face, pair]
        + [(value.shape, value.dtype) for value in inputs[8:]],
        [pltpu.VMEM(value.shape, value.dtype) for value in inputs[:8]]
        + work
        + [pltpu.SemaphoreType.DMA((len(inputs),))],
        inputs,
        pl.BlockSpec(memory_space=pl.ANY),
    )
    from_inner, from_outer = swap_faces(to_inner, to_outer)
    local, scale, to_inner, to_outer, terms = call(
        second_kernel,
        [padded, ((1, PADDED), F32), face, face, ((EVENTS, 4, LANES), F32)],
        [pltpu.VMEM(*padded), pltpu.VMEM(*pair)] + work,
        [
            from_inner,
            from_outer,
            wave,
            force,
            *kept[1:4],
            index,
            moduli,
            kept[0],
            earlier,
            *kept[4:],
        ],
    )
    from_inner, from_outer = swap_faces(to_inner, to_outer)
    terms = lax.all_to_all(terms, "event", 0, 0, tiled=True)
    forward, adjoint, kernels = call(
        third_kernel,
        [((3, 1, POINTS), F32), ((3, 1, POINTS), F32), ((2, 2, CUBE), F32)],
        [
            pltpu.VMEM(*padded),
            pltpu.VMEM((COARSE * 16, 6 * LANES), BF16),
            pltpu.VMEM((WIDE, 6 * LANES), BF16),
        ],
        [from_inner, from_outer, local, scale, index, terms],
    )
    return (rows(forward), rows(adjoint), kernels.transpose(0, 2, 1))


def solution(mesh):
    placed = (
        P("event", None, "mesh"),
        P("event", None, "mesh"),
        P("event", None, "mesh"),
        P("event", None, "mesh"),
        P(None, "mesh"),
        P("mesh", None),
        P("mesh", None),
        P(None, "mesh"),
        P(None, "mesh"),
        P("mesh"),
        P("mesh"),
        P("event", None, None, "mesh"),
    )
    return jax.shard_map(
        shards,
        mesh=mesh,
        in_specs=placed,
        out_specs=(
            P("event", None, "mesh"),
            P("event", None, "mesh"),
            P(None, None, ("mesh", "event")),
        ),
        check_vma=False,
    )
```

time: 331 us -> 51.5 us (0.16); the launches traced: 325 us -> 51.2 us
  other arithmetic: 131 us -> 0 us
  blocking collectives: 98.6 us -> 0 us
  local copies, waits for them, and re-layouts: 66.6 us -> 0 us
  starting transfers between devices: 17.3 us -> 31.6 us
  Pallas kernels: 0 us -> 9.89 us
  matrix products: 6 us -> 0 us
  waiting for transfers between devices: 3.77 us -> 9.02 us
    scatter-add x8 -> x0, other arithmetic: 120 us -> none  [the longest x4 70.2 us: shards(): forces = forces.at[:, :, lower].add(below).at[:, :, upper].add(above)]
    unnamed x1 -> x0, blocking collectives: 98.6 us -> none
    gather x6 -> x0, local copies, waits for them, and re-layouts: 38 us -> none  [the longest x2 28.3 us: collect(): jnp.take(waves.reshape(6, waves.shape[2]), columns.reshape(-1), axis=1)]
    all_to_all x0 -> x1, starting transfers between devices: none -> 18.3 us  [shards(): terms = lax.all_to_all(terms, 'event', 0, 0, tiled=True)]
    reshape x18 -> x0, local copies, waits for them, and re-layouts: 12.6 us -> none  [the longest x2 5.78 us: deposit(): return flat.reshape(2, 3, points)]
    pallas_call x0 -> x3, Pallas kernels: none -> 9.89 us  [call(): pl.pallas_call(kernel, out_shape=[jax.ShapeDtypeStruct(shape, dtype) for...]
    select_n x7 -> x0, other arithmetic: 8.51 us -> none  [the longest x3 7.13 us: collect(): jnp.take(waves.reshape(6, waves.shape[2]), columns.reshape(-1), axis=1)]
    unnamed x65 -> x0, local copies, waits for them, and re-layouts: 6.37 us -> none
  transfers between devices with their start and end apart: 4 -> 5, of which waited for: 1 -> 3; matrix products, arithmetic and copies ran while one was open for 15% -> 0% of each run, Pallas kernels for 0% -> 0%
where the time goes in v1:
time: 51.5 us; the launch traced here: 51.2 us
  starting transfers between devices  31.6 us (61%)
  Pallas kernels  9.89 us (19%)
  waiting for transfers between devices  9.02 us (18%)
  between operations  0.7 us (1%)
    all_to_all x1, starting transfers between devices, shards(): terms = lax.all_to_all(terms, 'event', 0, 0, tiled=True)  18.3 us
    pallas_call x3, Pallas kernels, call(): pl.pallas_call(kernel, out_shape=[jax.ShapeDtypeStruct(shape, dtype) for...  9.89 us
    ppermute x2, starting transfers between devices, swap_faces(): lax.ppermute(to_outer, 'mesh', outer)  9.47 us
    ppermute x2, waiting for transfers between devices, swap_faces(): lax.ppermute(to_outer, 'mesh', outer)  6.54 us
    ppermute x2, starting transfers between devices, swap_faces(): lax.ppermute(to_inner, 'mesh', inner)  3.84 us
    all_to_all x1, waiting for transfers between devices, shards(): terms = lax.all_to_all(terms, 'event', 0, 0, tiled=True)  2.48 us
  transfers between devices with their start and end apart: 5, of which 3 were waited for; matrix products, arithmetic and copies ran while one was open for 0% of the time, Pallas kernels for 0%

profile of v1, /device:TPU:32, one launch (start us, length us, event | category | flops | bytes accessed | tf_op | source)
XLA Modules:
  0.0 51.2 jit_solution(15935461854414944215)
XLA Ops:
  0.6 4.6 %shard_map.157 = (f32[8,2816]{1,0:T(8,128)S(1)}, f32[8,2816]{1,0:T(8,128)S(1)}, s32[48,128]{1,0:T(8,128)S(1)}, f32[64,128]{1,0:T(8,128)S(1)}, f32[24,128]{1,0:T(...) custom-call(f32[3,1,2601]{2,1,0:T(1,128)} %bitcast.14, ...), custom_call_target="tpu_custom_call" | custom-call | tf_op jit(solution)/shard_map/pallas_call | solution.py:310
  5.2 1.9 %collective-permute-start = (f32[24,128]{1,0:T(8,128)S(1)}, f32[24,128]{1,0:T(8,128)S(1)}, u32[]{:S(2)}, u32[]{:S(2)}) collective-permute-start(f32[24,128]{1,0:T(8,128)S(1)} %get-tuple-element.24), channel_id=1, source_target_pairs={{0,16},{16,0},{32,48},{48,32},{64,80},{80,64},{96,112},{112,96},{1... | collective-permute-start | bytes 36872 | tf_op jit(solution)/shard_map/ppermute | solution.py:324
  7.2 6.1 %collective-permute-start.1 = (f32[24,128]{1,0:T(8,128)S(1)}, f32[24,128]{1,0:T(8,128)S(1)}, u32[]{:S(2)}, u32[]{:S(2)}) collective-permute-start(f32[24,128]{1,0:T(8,128)S(1)} %get-tuple-element.25), channel_id=1, source_target_pairs={{16,32},{32,16},{48,64},{64,48},{80,96},{96,80},{112,128},{128,112... | collective-permute-start | bytes 36872 | tf_op jit(solution)/shard_map/ppermute | solution.py:324
  13.3 0.0 collective-permute-done.from_inner
  13.3 1.9 %collective-permute-done.1.from_outer = f32[24,128]{1,0:T(8,128)S(1)} collective-permute-done((f32[24,128]{1,0:T(8,128)S(1)}, f32[24,128]{1,0:T(8,128)S(1)}, u32[]{:S(2)}, u32[]{:S(2)}) %collective-permute-start.1) | collective-permute-done | bytes 12320 | tf_op jit(solution)/shard_map/ppermute | solution.py:324
  15.2 4.3 %shard_map.158 = (f32[8,2816]{1,0:T(8,128)S(1)}, f32[1,2816]{1,0:T(1,128)S(1)}, f32[24,128]{1,0:T(8,128)S(1)}, f32[24,128]{1,0:T(8,128)S(1)}, f32[16,4,128]{2,1,0:T(4,128)}) custom-call(f32[24,128]{1,0:T(8,128)S(1)} %collective-permute-done.from_inner, f32[24,128]{1,0:T(8,128)S(1)} %collective-permute-done.1.from_outer, ...), custom_call_target="tpu_custom_call" | custom-call | tf_op jit(solution)/shard_map/pallas_call | solution.py:310
  19.5 18.3 %all-to-all-start = ((f32[16,4,128]{2,1,0:T(4,128)}), f32[16,4,128]{2,1,0:T(4,128)S(1)}, u32[]{:S(2)}, u32[]{:S(2)}) async-start(f32[16,4,128]{2,1,0:T(4,128)} %get-tuple-element.41), calls=%async_computation | async-start | bytes 65536 | tf_op jit(solution)/shard_map/all_to_all | solution.py:400
  37.8 1.9 %collective-permute-start.2 = (f32[24,128]{1,0:T(8,128)S(1)}, f32[24,128]{1,0:T(8,128)S(1)}, u32[]{:S(2)}, u32[]{:S(2)}) collective-permute-start(f32[24,128]{1,0:T(8,128)S(1)} %get-tuple-element.37), channel_id=1, source_target_pairs={{0,16},{16,0},{32,48},{48,32},{64,80},{80,64},{96,112},{112,96},{1... | collective-permute-start | bytes 36872 | tf_op jit(solution)/shard_map/ppermute | solution.py:324
  39.7 3.4 %collective-permute-start.3 = (f32[24,128]{1,0:T(8,128)S(1)}, f32[24,128]{1,0:T(8,128)S(1)}, u32[]{:S(2)}, u32[]{:S(2)}) collective-permute-start(f32[24,128]{1,0:T(8,128)S(1)} %get-tuple-element.38), channel_id=1, source_target_pairs={{16,32},{32,16},{48,64},{64,48},{80,96},{96,80},{112,128},{128,112... | collective-permute-start | bytes 36872 | tf_op jit(solution)/shard_map/ppermute | solution.py:324
  43.1 0.0 collective-permute-done.2.from_inner
  43.1 4.6 %collective-permute-done.3.from_outer = f32[24,128]{1,0:T(8,128)S(1)} collective-permute-done((f32[24,128]{1,0:T(8,128)S(1)}, f32[24,128]{1,0:T(8,128)S(1)}, u32[]{:S(2)}, u32[]{:S(2)}) %collective-permute-start.3) | collective-permute-done | bytes 12320 | tf_op jit(solution)/shard_map/ppermute | solution.py:324
  47.8 2.5 %all-to-all-done.terms = f32[16,4,128]{2,1,0:T(4,128)S(1)} async-done(((f32[16,4,128]{2,1,0:T(4,128)}), f32[16,4,128]{2,1,0:T(4,128)S(1)}, u32[]{:S(2)}, u32[]{:S(2)}) %all-to-all-start) | async-done | bytes 32800 | tf_op jit(solution)/shard_map/all_to_all | solution.py:400
  50.2 1.0 %shard_map.159 = (f32[3,1,2601]{2,1,0:T(1,128)}, f32[3,1,2601]{2,1,0:T(1,128)}, f32[2,2,125]{2,1,0:T(2,128)}) custom-call(f32[24,128]{1,0:T(8,128)S(1)} %collective-permute-done.2.from_inner, f32[24,128]{1,0:T(8,128)S(1)} %collective-permute-done.3.from_outer, f32[8,2816]{1,0:T(8,128)S(1)} %get-tuple-element.39.local, ...), custom_call_target="tpu_custom_call" | custom-call | tf_op jit(solution)/shard_map/pallas_call | solution.py:310
Async XLA Ops:
  5.2 8.0 %collective-permute-start = (f32[24,128]{1,0:T(8,128)S(1)}, f32[24,128]{1,0:T(8,128)S(1)}, u32[]{:S(2)}, u32[]{:S(2)}) collective-permute-start(f32[24,128]{1,0:T(8,128)S(1)} %get-tuple-element.24), channel_id=1, source_target_pairs={{0,16},{16,0},{32,48},{48,32},{64,80},{80,64},{96,112},{112,96},{1... | collective-permute-start | bytes 36872 | tf_op jit(solution)/shard_map/ppermute | solution.py:324
  7.2 8.0 %collective-permute-start.1 = (f32[24,128]{1,0:T(8,128)S(1)}, f32[24,128]{1,0:T(8,128)S(1)}, u32[]{:S(2)}, u32[]{:S(2)}) collective-permute-start(f32[24,128]{1,0:T(8,128)S(1)} %get-tuple-element.25), channel_id=1, source_target_pairs={{16,32},{32,16},{48,64},{64,48},{80,96},{96,80},{112,128},{128,112... | collective-permute-start | bytes 36872 | tf_op jit(solution)/shard_map/ppermute | solution.py:324
  19.5 30.7 %all-to-all-start = ((f32[16,4,128]{2,1,0:T(4,128)}), f32[16,4,128]{2,1,0:T(4,128)S(1)}, u32[]{:S(2)}, u32[]{:S(2)}) async-start(f32[16,4,128]{2,1,0:T(4,128)} %get-tuple-element.41), calls=%async_computation | async-start | bytes 65536 | tf_op jit(solution)/shard_map/all_to_all | solution.py:400
  37.8 5.3 %collective-permute-start.2 = (f32[24,128]{1,0:T(8,128)S(1)}, f32[24,128]{1,0:T(8,128)S(1)}, u32[]{:S(2)}, u32[]{:S(2)}) collective-permute-start(f32[24,128]{1,0:T(8,128)S(1)} %get-tuple-element.37), channel_id=1, source_target_pairs={{0,16},{16,0},{32,48},{48,32},{64,80},{80,64},{96,112},{112,96},{1... | collective-permute-start | bytes 36872 | tf_op jit(solution)/shard_map/ppermute | solution.py:324
  39.7 8.0 %collective-permute-start.3 = (f32[24,128]{1,0:T(8,128)S(1)}, f32[24,128]{1,0:T(8,128)S(1)}, u32[]{:S(2)}, u32[]{:S(2)}) collective-permute-start(f32[24,128]{1,0:T(8,128)S(1)} %get-tuple-element.38), channel_id=1, source_target_pairs={{16,32},{32,16},{48,64},{64,48},{80,96},{96,80},{112,128},{128,112... | collective-permute-start | bytes 36872 | tf_op jit(solution)/shard_map/ppermute | solution.py:324

commit v2 on v1

v2 whole, which is shorter than its diff:
```python
import functools
import math

import jax
import jax.numpy as jnp
import numpy as np
from jax import lax
from jax.experimental import pallas as pl
from jax.experimental.pallas import tpu as pltpu
from jax.sharding import PartitionSpec as P

F32 = jnp.float32
BF16 = jnp.bfloat16
EVENTS = 16
FIELDS = 6
ELEMS = 32
CUBE = 125
POINTS = 2601
FACE = 289
LANES = 128
WIDE = 256
FINE = 21
COARSE = 11
PADDED = COARSE * WIDE
HALF = 16
RECEIVER_ROW = 32
FACE_ROW = 40
SLOT_ROW = 6
FACES = 24
PARITY_ROW = 46
KERNEL_WEIGHT = 0.02

VMEM = pl.BlockSpec(memory_space=pltpu.VMEM)
MIB = 1024 * 1024


def derivative_table():
    root = math.sqrt(3.0 / 7.0)
    points = [-1.0, -root, 0.0, root, 1.0]
    legendre = [(35.0 * x**4 - 30.0 * x**2 + 3.0) / 8.0 for x in points]
    table = np.zeros((5, 5))
    for row in range(5):
        for column in range(5):
            if row != column:
                table[row, column] = (
                    legendre[row] / legendre[column] / (points[row] - points[column])
                )
    table[0, 0] = -2.5
    table[4, 4] = 2.5
    return table


def cube_tables():
    deriv = derivative_table().astype(np.float32).astype(np.float64)
    line = np.array([0.1, 49.0 / 90.0, 32.0 / 45.0, 49.0 / 90.0, 0.1])
    cube = (line[:, None, None] * line[None, :, None] * line[None, None, :]).reshape(CUBE)
    cube = cube.astype(np.float32).astype(np.float64)
    along = [
        np.kron(np.eye(25), deriv),
        np.kron(np.eye(5), np.kron(deriv, np.eye(5))),
        np.kron(deriv, np.eye(25)),
    ]
    ahead = np.zeros((3 * LANES, LANES))
    back = np.zeros((3 * LANES, LANES))
    for i in range(3):
        ahead[i * LANES : i * LANES + CUBE, :CUBE] = along[i]
        back[i * LANES : i * LANES + CUBE, :CUBE] = -cube[:, None] * along[i]
    return (jnp.asarray(ahead, F32), jnp.asarray(back, F32))


def split(value):
    high = value.astype(BF16)
    return (high, (value - high.astype(F32)).astype(BF16))


def product(value, table, side):
    high, low = split(value)
    table_high, table_low = split(table)

    def dot(a, b):
        return lax.dot_general(a, b, (((1,), (side,)), ((), ())), preferred_element_type=F32)

    return dot(high, table_high) + (dot(low, table_high) + dot(high, table_low))


def pick(row, lanes):
    return jnp.take_along_axis(row, lanes, axis=1, mode="promise_in_bounds")


def gather_elements(wave_ref, index_ref, count):
    groups = []
    for t in range(0, ELEMS, 8):
        index = index_ref[t : t + 8, :]
        fine = index >> 7
        lane = index & 127
        found = [jnp.zeros((8, LANES), F32) for _ in range(count)]
        for c in range(FINE):
            hit = fine == c
            for r in range(count):
                row = wave_ref[r : r + 1, c * LANES : (c + 1) * LANES]
                found[r] = jnp.where(hit, pick(jnp.broadcast_to(row, (8, LANES)), lane), found[r])
        groups.append(found)
    return [jnp.concatenate(parts, 0) for parts in zip(*groups)]


def gather_faces(blocks, index_ref, targets):
    for face in range(2):
        for tile in range(3):
            at = FACE_ROW + 3 * face + tile
            index = jnp.broadcast_to(index_ref[at : at + 1, :], (8, LANES))
            fine = index >> 7
            lane = index & 127
            found = jnp.zeros((8, LANES), F32)
            for c in range(FINE):
                part = slice((c % 2) * LANES, (c % 2 + 1) * LANES)
                found = jnp.where(fine == c, pick(blocks[c // 2][:, part], lane), found)
            targets[face][8 * tile : 8 * tile + 8, :] = found


def scatter(tiles, rows, left_ref, right_ref):
    step = lax.broadcasted_iota(jnp.int32, (16, LANES), 0)
    for t, (tile, row) in enumerate(zip(tiles, rows)):
        lanes = slice(t * LANES, (t + 1) * LANES)
        index = jnp.broadcast_to(row, (16, LANES))
        coarse = (index >> 8).astype(F32).astype(BF16)
        offset = ((index & 255) - step).astype(F32).astype(BF16)
        high = tile.astype(BF16).astype(F32)
        both = jnp.concatenate([high, tile - high], 0).astype(BF16)
        for c in range(COARSE):
            left_ref[c * 16 : (c + 1) * 16, lanes] = jnp.where(coarse == c, both, jnp.zeros_like(both))
        for c in range(16):
            right_ref[c * 16 : (c + 1) * 16, lanes] = jnp.where(
                offset == c * 16, jnp.ones_like(both), jnp.zeros_like(both)
            )
    width = len(rows) * LANES
    total = lax.dot_general(
        left_ref[:, :width],
        right_ref[:, :width],
        (((1,), (1,)), ((), ())),
        preferred_element_type=F32,
    )
    return [total[c * 16 : c * 16 + 8] + total[c * 16 + 8 : c * 16 + 16] for c in range(COARSE)]


def strains(fields, ahead):
    count = fields[0].shape[0]
    grads = product(jnp.concatenate(fields, 0), ahead, 1)

    def grad(f, i, j):
        r = (3 * f + j) * count
        return grads[r : r + count, i * LANES : (i + 1) * LANES]

    result = []
    for f in range(2):
        normal = [grad(f, i, i) for i in range(3)]
        dilation = normal[0] + normal[1] + normal[2]
        deviator = [n - dilation * (1.0 / 3.0) for n in normal]
        shear = {
            (i, j): 0.5 * (grad(f, i, j) + grad(f, j, i)) for i, j in ((0, 1), (0, 2), (1, 2))
        }
        result.append((dilation, deviator, shear))
    return result


def kernel_terms(strained, kappa, shear_mod):
    (dilation0, normal0, shear0), (dilation1, normal1, shear1) = strained
    bulk = -KERNEL_WEIGHT * kappa * dilation0 * dilation1
    inner = normal0[0] * normal1[0] + normal0[1] * normal1[1] + normal0[2] * normal1[2]
    cross = sum(shear0[key] * shear1[key] for key in shear0)
    return (bulk, -2.0 * KERNEL_WEIGHT * shear_mod * (inner + 2.0 * cross))


def element_forces(strained, kappa, shear_mod, back):
    twice = 2.0 * shear_mod
    columns = []
    for dilation, deviator, shear in strained:
        pressure = kappa * dilation
        for j in range(3):
            stress = [
                pressure + twice * deviator[j] if i == j else twice * shear[min(i, j), max(i, j)]
                for i in range(3)
            ]
            columns.append(jnp.concatenate(stress, 1))
    return product(jnp.concatenate(columns, 0), back, 0)


def element_tiles(tile_ref, forces, source_ref, step):
    count = forces.shape[0] // FIELDS
    tile_ref[...] = jnp.zeros_like(tile_ref)
    for r in range(FIELDS):
        tile_ref[pl.ds(r, count, stride=8), :] = forces[r * count : (r + 1) * count]
    for j in range(3):
        row = count * 8 + 3 + j
        tile_ref[row : row + 1, :] = source_ref[j, step : step + 1, :]
    return [tile_ref[8 * t : 8 * t + 8, :] for t in range(count + 1)]


def block(c):
    return slice(c * WIDE, (c + 1) * WIDE)


def even_partition():
    return lax.rem(lax.axis_index("mesh"), 2) == 0


def halves_in_order(value, even):
    first, second = value[:HALF], value[HALF:]
    return [jnp.where(even, second, first), jnp.where(even, first, second)]


def first_kernel(*refs):
    inputs, refs = refs[:14], refs[14:]
    wave, force, index, moduli, to_inner, to_outer, totals = refs[:7]
    forward_prev, adjoint_prev, step_scale, source, ahead, back = kept = refs[7:13]
    arrived = refs[13:21]
    tiles, left, right, sems = refs[21:]
    copies = [
        pltpu.make_async_copy(value, target, sems.at[i])
        for i, (value, target) in enumerate(zip(inputs, arrived + kept))
    ]
    for i in (2, 0, 1, 6, 7, 12, 13, 4, 5, 3, 11, 8, 9, 10):
        copies[i].start()
    forward, adjoint, connectivity, receivers, lower, upper, bulk_modulus, shear_modulus = arrived
    for ref in (wave, moduli):
        ref[...] = jnp.zeros_like(ref)
    index[0:FACE_ROW, :] = jnp.zeros((FACE_ROW, LANES), jnp.int32)
    index[FACE_ROW:, :] = jnp.full((8, LANES), -1, jnp.int32)
    for copy in copies[:8]:
        copy.wait()
    for j in range(3):
        wave[j : j + 1, 0:POINTS] = forward[j]
        wave[3 + j : 4 + j, 0:POINTS] = adjoint[j]
    even = even_partition()
    for face, (part, kappa, shear_mod) in enumerate(
        zip(*(halves_in_order(ref[...], even) for ref in (connectivity, bulk_modulus, shear_modulus)))
    ):
        start = face * HALF
        index[start : start + HALF, 0:CUBE] = part
        moduli[start : start + HALF, 0:CUBE] = kappa
        moduli[ELEMS + start : ELEMS + start + HALF, 0:CUBE] = shear_mod
    index[RECEIVER_ROW : RECEIVER_ROW + 1, :] = receivers[...]
    index[PARITY_ROW : PARITY_ROW + 1, :] = jnp.where(even, jnp.ones((1, LANES), jnp.int32), 0)
    faces = (jnp.where(even, upper[...], lower[...]), jnp.where(even, lower[...], upper[...]))
    for t in range(3):
        size = min(LANES, FACE - t * LANES)
        for face in range(2):
            at = FACE_ROW + 3 * face + t
            index[at : at + 1, 0:size] = faces[face][:, t * LANES : t * LANES + size]
    kappa = moduli[0:ELEMS, :]
    shear_mod = moduli[ELEMS : 2 * ELEMS, :]
    fields = gather_elements(wave, index, FIELDS)
    for copy in copies[11:]:
        copy.wait()
    strained = strains(fields, ahead[...])
    bulk, shear = kernel_terms(strained, kappa, shear_mod)
    totals[0:ELEMS, :] = bulk
    totals[ELEMS : 2 * ELEMS, :] = shear
    values = element_tiles(tiles, element_forces(strained, kappa, shear_mod, back[...]), source, 0)
    forces = scatter(values, [index[t : t + 1, :] for t in range(RECEIVER_ROW + 1)], left, right)
    gather_faces(forces, index, (to_inner, to_outer))
    for c in range(COARSE):
        force[:, block(c)] = forces[c]
    for copy in copies[8:11]:
        copy.wait()


def between_kernel(
    wave, force, forward_prev, adjoint_prev, step_scale, index, local, scale, fields, slots, at_inner, at_outer, left, right
):
    scale[...] = jnp.zeros_like(scale)
    local[...] = jnp.zeros_like(local)
    scale[0:1, 0:POINTS] = step_scale[...].reshape(1, POINTS)
    for j in range(3):
        local[j : j + 1, 0:POINTS] = forward_prev[j]
        local[3 + j : 4 + j, 0:POINTS] = adjoint_prev[j]
    row = lax.broadcasted_iota(jnp.int32, (8, LANES), 0)
    lane = lax.broadcasted_iota(jnp.int32, (8, LANES), 1)
    marks = [jnp.where(row == SLOT_ROW, lane + (t * LANES + 1), 0).astype(F32) for t in range(3)]
    rows = [index[FACE_ROW + t : FACE_ROW + t + 1, :] for t in range(6)]
    marked = scatter(marks + marks, rows, left, right)
    wide_row = lax.broadcasted_iota(jnp.int32, (8, WIDE), 0)
    spread = []
    for c in range(COARSE):
        spread.append(jnp.broadcast_to(scale[0:1, block(c)], (8, WIDE)))
        local[:, block(c)] = jnp.where(
            wide_row == SLOT_ROW,
            marked[c],
            2.0 * wave[:, block(c)] - local[:, block(c)] + spread[c] * force[:, block(c)],
        )
    gather_faces(spread, index, (at_inner, at_outer))
    found = gather_elements(local, index, FIELDS + 1)
    for r in range(FIELDS):
        fields[r * ELEMS : (r + 1) * ELEMS, :] = found[r]
    slots[...] = found[SLOT_ROW].astype(jnp.int32) - 1


def second_kernel(
    from_inner, scaled_outer, fields, slots, factors, moduli, earlier, ahead, index, terms, now, sums
):
    added = []
    for face, value in enumerate((factors[...] * from_inner[...], scaled_outer[...])):
        scaled = [value[8 * t : 8 * t + 8, :] for t in range(3)]
        fine = slots[face * HALF : (face + 1) * HALF, :] >> 7
        lane = slots[face * HALF : (face + 1) * HALF, :] & 127
        values = []
        for r in range(FIELDS):
            start = r * ELEMS + face * HALF
            value = fields[start : start + HALF, :]
            for t in range(3):
                got = pick(jnp.broadcast_to(scaled[t][r : r + 1, :], (HALF, LANES)), lane)
                value = value + jnp.where(fine == t, got, 0.0)
            values.append(value)
        added.append(values)
    values = [jnp.concatenate(pair, 0) for pair in zip(*added)]
    for r in range(FIELDS):
        now[r * ELEMS : (r + 1) * ELEMS, :] = values[r]
    found = kernel_terms(strains(values, ahead[...]), moduli[0:ELEMS, :], moduli[ELEMS : 2 * ELEMS, :])
    even = jnp.broadcast_to(index[PARITY_ROW : PARITY_ROW + 1, :], (HALF, LANES)) == 1
    for which in range(2):
        start = which * ELEMS
        total = earlier[start : start + ELEMS, :] + found[which]
        sums[start : start + ELEMS, :] = jnp.concatenate(halves_in_order(total, even), 0)
    for which in range(2):
        for e in range(2):
            terms[:, 2 * which + e, :] = sums[pl.ds(which * ELEMS + e, EVENTS, stride=2), :]


def third_kernel(
    now, moduli, index, source, ahead, back, wave, local, scale, following, to_inner, to_outer, tiles, left, right
):
    strained = strains([now[r * ELEMS : (r + 1) * ELEMS, :] for r in range(FIELDS)], ahead[...])
    forces = element_forces(strained, moduli[0:ELEMS, :], moduli[ELEMS : 2 * ELEMS, :], back[...])
    values = element_tiles(tiles, forces, source, 1)
    forces = scatter(values, [index[t : t + 1, :] for t in range(RECEIVER_ROW + 1)], left, right)
    gather_faces(forces, index, (to_inner, to_outer))
    for c in range(COARSE):
        following[:, block(c)] = (
            2.0 * local[:, block(c)] - wave[:, block(c)] + scale[0:1, block(c)] * forces[c]
        )


def fourth_kernel(
    first_inner, from_inner, first_outer, from_outer, following, scale, index, forward, adjoint, result, left, right
):
    inner = 2.0 * first_inner[...] + from_inner[...]
    outer = 2.0 * first_outer[...] + from_outer[...]
    values = [value[8 * t : 8 * t + 8, :] for value in (inner, outer) for t in range(3)]
    added = scatter(values, [index[FACE_ROW + t : FACE_ROW + t + 1, :] for t in range(6)], left, right)
    for c in range(COARSE):
        result[:, block(c)] = following[:, block(c)] + scale[0:1, block(c)] * added[c]
    for j in range(3):
        forward[j] = result[j : j + 1, 0:POINTS]
        adjoint[j] = result[3 + j : 4 + j, 0:POINTS]


def call(kernel, outs, scratch, args, place=VMEM):
    return pl.pallas_call(
        kernel,
        out_shape=[jax.ShapeDtypeStruct(shape, dtype) for shape, dtype in outs],
        in_specs=[place] * len(args),
        out_specs=[VMEM] * len(outs),
        scratch_shapes=scratch,
        compiler_params=pltpu.CompilerParams(vmem_limit_bytes=24 * MIB),
    )(*args)


def swap_faces(to_inner, to_outer):
    count = lax.axis_size("mesh")
    inner = [(i, i ^ 1) for i in range(count)]
    outer = [(i, i + 1 if i % 2 else i - 1) for i in range(1, count - 1)]
    from_outer = lax.ppermute(to_outer, "mesh", outer)
    return (lax.ppermute(to_inner, "mesh", inner), from_outer)


def scatter_work(tiles):
    return [
        pltpu.VMEM((COARSE * 16, tiles * LANES), BF16),
        pltpu.VMEM((WIDE, tiles * LANES), BF16),
    ]


def shards(
    forward_now,
    forward_prev,
    adjoint_now,
    adjoint_prev,
    connectivity,
    lower_face,
    upper_face,
    bulk_modulus,
    shear_modulus,
    step_scale,
    receiver_points,
    adjoint_source,
):
    def rows(field):
        return field.transpose(1, 0, 2)

    padded = ((8, PADDED), F32)
    face = ((FACES, LANES), F32)
    pair = ((2 * ELEMS, LANES), F32)
    at_elements = ((FIELDS * ELEMS, LANES), F32)
    tiles = pltpu.VMEM(((ELEMS + 1) * 8, LANES), F32)
    inputs = [
        rows(forward_now),
        rows(adjoint_now),
        connectivity.T,
        receiver_points.reshape(1, LANES),
        lower_face,
        upper_face,
        bulk_modulus.T,
        shear_modulus.T,
        rows(forward_prev),
        rows(adjoint_prev),
        step_scale,
        adjoint_source[0].transpose(1, 0, 2),
        *cube_tables(),
    ]
    inputs = [pltpu.with_memory_space_constraint(value, pltpu.HBM) for value in inputs]
    wave, force, index, moduli, to_inner, to_outer, earlier, *kept = call(
        first_kernel,
        [padded, padded, ((48, LANES), jnp.int32), pair, face, face, pair]
        + [(value.shape, value.dtype) for value in inputs[8:]],
        [pltpu.VMEM(value.shape, value.dtype) for value in inputs[:8]]
        + [tiles]
        + scatter_work(ELEMS + 1)
        + [pltpu.SemaphoreType.DMA((len(inputs),))],
        inputs,
        pl.BlockSpec(memory_space=pl.ANY),
    )
    forward_prev, adjoint_prev, step_scale, source, ahead, back = kept
    first_inner, first_outer = swap_faces(to_inner, to_outer)
    local, scale, fields, slots, at_inner, at_outer = call(
        between_kernel,
        [padded, ((1, PADDED), F32), at_elements, ((ELEMS, LANES), jnp.int32), face, face],
        scatter_work(6),
        [wave, force, forward_prev, adjoint_prev, step_scale, index],
    )
    terms, now = call(
        second_kernel,
        [((EVENTS, 4, LANES), F32), at_elements],
        [pltpu.VMEM(*pair)],
        [first_inner, at_outer * first_outer, fields, slots, at_inner, moduli, earlier, ahead, index],
    )
    terms = lax.all_to_all(terms, "event", 0, 0, tiled=True)
    following, to_inner, to_outer = call(
        third_kernel,
        [padded, face, face],
        [tiles] + scatter_work(ELEMS + 1),
        [now, moduli, index, source, ahead, back, wave, local, scale],
    )
    from_inner, from_outer = swap_faces(to_inner, to_outer)
    forward, adjoint = call(
        fourth_kernel,
        [((3, 1, POINTS), F32), ((3, 1, POINTS), F32)],
        [pltpu.VMEM(*padded)] + scatter_work(6),
        [first_inner, from_inner, first_outer, from_outer, following, scale, index],
    )
    kernels = jnp.sum(terms, axis=0)[:, :CUBE].reshape(2, 2, CUBE)
    return (rows(forward), rows(adjoint), kernels.transpose(0, 2, 1))


def solution(mesh):
    placed = (
        P("event", None, "mesh"),
        P("event", None, "mesh"),
        P("event", None, "mesh"),
        P("event", None, "mesh"),
        P(None, "mesh"),
        P("mesh", None),
        P("mesh", None),
        P(None, "mesh"),
        P(None, "mesh"),
        P("mesh"),
        P("mesh"),
        P("event", None, None, "mesh"),
    )
    return jax.shard_map(
        shards,
        mesh=mesh,
        in_specs=placed,
        out_specs=(
            P("event", None, "mesh"),
            P("event", None, "mesh"),
            P(None, None, ("mesh", "event")),
        ),
        check_vma=False,
    )
```

time: 51.5 us -> 45.9 us (0.89)
  the two profiles are of different devices: /device:TPU:32 before, /device:TPU:34 now
where the time goes in v2:
time: 45.9 us; the launch traced here: 45.6 us
  starting transfers between devices  30.3 us (66%)
  Pallas kernels  8.71 us (19%)
  waiting for transfers between devices  5.26 us (11%)
  between operations  0.71 us (2%)
  other arithmetic  0.61 us (1%)
    all_to_all x1, starting transfers between devices, shards(): terms = lax.all_to_all(terms, 'event', 0, 0, tiled=True)  18.3 us
    pallas_call x5, Pallas kernels, call(): pl.pallas_call(kernel, out_shape=[jax.ShapeDtypeStruct(shape, dtype) for...  8.71 us
    ppermute x2, starting transfers between devices, swap_faces(): from_outer = lax.ppermute(to_outer, 'mesh', outer)  8.24 us
    ppermute x2, waiting for transfers between devices, swap_faces(): from_outer = lax.ppermute(to_outer, 'mesh', outer)  5.18 us
    ppermute x2, starting transfers between devices, swap_faces(): return (lax.ppermute(to_inner, 'mesh', inner), from_outer)  3.84 us
  transfers between devices with their start and end apart: 5, of which 2 were waited for; matrix products, arithmetic and copies ran while one was open for 0% of the time, Pallas kernels for 9%

profile of v2, /device:TPU:34, one launch (start us, length us, event | category | flops | bytes accessed | tf_op | source)
XLA Modules:
  0.0 45.6 jit_solution(6112674694792985479)
XLA Ops:
  0.6 3.7 %shard_map.157 = (f32[8,2816]{1,0:T(8,128)S(1)}, f32[8,2816]{1,0:T(8,128)S(1)}, s32[48,128]{1,0:T(8,128)S(1)}, f32[64,128]{1,0:T(8,128)S(1)}, f32[24,128]{1,0:T(...) custom-call(f32[3,1,2601]{2,1,0:T(1,128)} %bitcast.17, ...), custom_call_target="tpu_custom_call" | custom-call | tf_op jit(solution)/shard_map/pallas_call | solution.py:357
  4.3 5.4 %collective-permute-start.1 = (f32[24,128]{1,0:T(8,128)S(1)}, f32[24,128]{1,0:T(8,128)S(1)}, u32[]{:S(2)}, u32[]{:S(2)}) collective-permute-start(f32[24,128]{1,0:T(8,128)S(1)} %get-tuple-element.37), channel_id=1, source_target_pairs={{16,32},{32,16},{48,64},{64,48},{80,96},{96,80},{112,128},{128,112... | collective-permute-start | bytes 36872 | tf_op jit(solution)/shard_map/ppermute | solution.py:371
  9.8 1.9 %collective-permute-start = (f32[24,128]{1,0:T(8,128)S(1)}, f32[24,128]{1,0:T(8,128)S(1)}, u32[]{:S(2)}, u32[]{:S(2)}) collective-permute-start(f32[24,128]{1,0:T(8,128)S(1)} %get-tuple-element.29), channel_id=1, source_target_pairs={{0,16},{16,0},{32,48},{48,32},{64,80},{80,64},{96,112},{112,96},{1... | collective-permute-start | bytes 36872 | tf_op jit(solution)/shard_map/ppermute | solution.py:372
  11.7 1.0 %shard_map.158 = (f32[8,2816]{1,0:T(8,128)S(1)}, f32[1,2816]{1,0:T(1,128)S(1)}, f32[192,128]{1,0:T(8,128)S(1)}, s32[32,128]{1,0:T(8,128)S(1)}, f32[24,128]{1,0:T(8,128)S(1)}, /*index=5*/f32[24,128]{1,0:T(8,128)S(1)}) custom-call(f32[8,2816]{1,0:T(8,128)S(1)} %get-tuple-element.30.wave, f32[8,2816]{1,0:T(8,128)S(1)} %get-tuple-element.31.force, ...), custom_call_target="tpu_custom_call" | custom-call | tf_op jit(solution)/shard_map/pallas_call | solution.py:357
  12.7 0.0 collective-permute-done.1.first_outer
  12.8 0.1 collective-permute-done.from_inner.first_inner
  12.8 1.1 %shard_map.159 = (f32[16,4,128]{2,1,0:T(4,128)}, f32[192,128]{1,0:T(8,128)S(1)}) custom-call(f32[24,128]{1,0:T(8,128)S(1)} %collective-permute-done.from_inner.first_inner, f32[24,128]{1,0:T(8,128)S(1)} %mul.3.scaled_outer, f32[192,128]{1,0:T(8,128)S(1)} %get-tuple-element.38.fields, s32[32,128]{1,0:T(8,128)S(1)} %get-tuple-element.39.slots, ...), custom_call_target="tpu_custom_call" | custom-call | tf_op jit(solution)/shard_map/pallas_call | solution.py:357
  13.9 18.3 %all-to-all-start = ((f32[16,4,128]{2,1,0:T(4,128)}), f32[16,4,128]{2,1,0:T(4,128)S(1)}, u32[]{:S(2)}, u32[]{:S(2)}) async-start(f32[16,4,128]{2,1,0:T(4,128)} %get-tuple-element.54), calls=%async_computation | async-start | bytes 65536 | tf_op jit(solution)/shard_map/all_to_all | solution.py:445
  32.2 1.9 %shard_map.160 = (f32[8,2816]{1,0:T(8,128)S(1)}, f32[24,128]{1,0:T(8,128)S(1)}, f32[24,128]{1,0:T(8,128)S(1)}) custom-call(f32[192,128]{1,0:T(8,128)S(1)} %get-tuple-element.44.now, f32[64,128]{1,0:T(8,128)S(1)} %get-tuple-element.41.moduli, s32[48,128]{1,0:T(8,128)S(1)} %get-tuple-element.35.index, f32[3,2,128]{2,1,0:T(2,128)S(1)} %get-tuple-element.45.source, ...), custom_call_target="tpu_custom_call" | custom-call | tf_op jit(solution)/shard_map/pallas_call | solution.py:357
  34.1 1.9 %collective-permute-start.2 = (f32[24,128]{1,0:T(8,128)S(1)}, f32[24,128]{1,0:T(8,128)S(1)}, u32[]{:S(2)}, u32[]{:S(2)}) collective-permute-start(f32[24,128]{1,0:T(8,128)S(1)} %get-tuple-element.49), channel_id=1, source_target_pairs={{0,16},{16,0},{32,48},{48,32},{64,80},{80,64},{96,112},{112,96},{1... | collective-permute-start | bytes 36872 | tf_op jit(solution)/shard_map/ppermute | solution.py:372
  36.0 2.8 %collective-permute-start.3 = (f32[24,128]{1,0:T(8,128)S(1)}, f32[24,128]{1,0:T(8,128)S(1)}, u32[]{:S(2)}, u32[]{:S(2)}) collective-permute-start(f32[24,128]{1,0:T(8,128)S(1)} %get-tuple-element.50), channel_id=1, source_target_pairs={{16,32},{32,16},{48,64},{64,48},{80,96},{96,80},{112,128},{128,112... | collective-permute-start | bytes 36872 | tf_op jit(solution)/shard_map/ppermute | solution.py:371
  38.9 0.0 collective-permute-done.2.from_inner
  38.9 5.2 %collective-permute-done.3.from_outer = f32[24,128]{1,0:T(8,128)S(1)} collective-permute-done((f32[24,128]{1,0:T(8,128)S(1)}, f32[24,128]{1,0:T(8,128)S(1)}, u32[]{:S(2)}, u32[]{:S(2)}) %collective-permute-start.3) | collective-permute-done | bytes 12320 | tf_op jit(solution)/shard_map/ppermute | solution.py:371
  44.1 1.0 %shard_map.161 = (f32[3,1,2601]{2,1,0:T(1,128)}, f32[3,1,2601]{2,1,0:T(1,128)}) custom-call(f32[24,128]{1,0:T(8,128)S(1)} %collective-permute-done.from_inner.first_inner, f32[24,128]{1,0:T(8,128)S(1)} %collective-permute-done.2.from_inner, f32[24,128]{1,0:T(8,128)S(1)} %collective-permute-done.1.first_outer, ...), custom_call_target="tpu_custom_call" | custom-call | tf_op jit(solution)/shard_map/pallas_call | solution.py:357
  45.0 0.0 all-to-all-done
  45.0 0.6 %reduce_sum.9 = f32[4,128]{1,0:T(4,128)} reduce(f32[16,4,128]{2,1,0:T(4,128)S(1)} %all-to-all-done, f32[]{:T(128)} %constant.2.clone.1), dimensions={0}, to_apply=%region_0.0 | reduce | flops 7680 | bytes 34820 | tf_op jit(solution)/shard_map/reduce_sum | solution.py:459
  (1 shorter events, 0.0 us)
Async XLA Ops:
  4.3 8.4 %collective-permute-start.1 = (f32[24,128]{1,0:T(8,128)S(1)}, f32[24,128]{1,0:T(8,128)S(1)}, u32[]{:S(2)}, u32[]{:S(2)}) collective-permute-start(f32[24,128]{1,0:T(8,128)S(1)} %get-tuple-element.37), channel_id=1, source_target_pairs={{16,32},{32,16},{48,64},{64,48},{80,96},{96,80},{112,128},{128,112... | collective-permute-start | bytes 36872 | tf_op jit(solution)/shard_map/ppermute | solution.py:371
  9.8 3.1 %collective-permute-start = (f32[24,128]{1,0:T(8,128)S(1)}, f32[24,128]{1,0:T(8,128)S(1)}, u32[]{:S(2)}, u32[]{:S(2)}) collective-permute-start(f32[24,128]{1,0:T(8,128)S(1)} %get-tuple-element.29), channel_id=1, source_target_pairs={{0,16},{16,0},{32,48},{48,32},{64,80},{80,64},{96,112},{112,96},{1... | collective-permute-start | bytes 36872 | tf_op jit(solution)/shard_map/ppermute | solution.py:372
  13.9 31.1 %all-to-all-start = ((f32[16,4,128]{2,1,0:T(4,128)}), f32[16,4,128]{2,1,0:T(4,128)S(1)}, u32[]{:S(2)}, u32[]{:S(2)}) async-start(f32[16,4,128]{2,1,0:T(4,128)} %get-tuple-element.54), calls=%async_computation | async-start | bytes 65536 | tf_op jit(solution)/shard_map/all_to_all | solution.py:445
  34.1 4.8 %collective-permute-start.2 = (f32[24,128]{1,0:T(8,128)S(1)}, f32[24,128]{1,0:T(8,128)S(1)}, u32[]{:S(2)}, u32[]{:S(2)}) collective-permute-start(f32[24,128]{1,0:T(8,128)S(1)} %get-tuple-element.49), channel_id=1, source_target_pairs={{0,16},{16,0},{32,48},{48,32},{64,80},{80,64},{96,112},{112,96},{1... | collective-permute-start | bytes 36872 | tf_op jit(solution)/shard_map/ppermute | solution.py:372
  36.0 8.0 %collective-permute-start.3 = (f32[24,128]{1,0:T(8,128)S(1)}, f32[24,128]{1,0:T(8,128)S(1)}, u32[]{:S(2)}, u32[]{:S(2)}) collective-permute-start(f32[24,128]{1,0:T(8,128)S(1)} %get-tuple-element.50), channel_id=1, source_target_pairs={{16,32},{32,16},{48,64},{64,48},{80,96},{96,80},{112,128},{128,112... | collective-permute-start | bytes 36872 | tf_op jit(solution)/shard_map/ppermute | solution.py:371

commit v3 on v2

v3 whole, which is shorter than its diff:
```python
import functools
import math

import jax
import jax.numpy as jnp
import numpy as np
from jax import lax
from jax.experimental import pallas as pl
from jax.experimental.pallas import tpu as pltpu
from jax.sharding import PartitionSpec as P

F32 = jnp.float32
BF16 = jnp.bfloat16
EVENTS = 16
FIELDS = 6
ELEMS = 32
CUBE = 125
POINTS = 2601
FACE = 289
LANES = 128
WIDE = 256
FINE = 21
COARSE = 11
PADDED = COARSE * WIDE
HALF = 16
RECEIVER_ROW = 32
FACE_ROW = 40
PARITY_ROW = 46
SLOT_ROW = 6
SCALE_ROW = 7
OUTER = 512
ORDER = [8, 9, 10, 11, 12, 13, 14, 15, 0, 1, 2, 3, 4, 5, 6, 7]
SENT_KAPPA = FIELDS * HALF
SENT_SHEAR = SENT_KAPPA + HALF
SENT_SLOTS = SENT_SHEAR + HALF
SENT_FACE = SENT_SLOTS + HALF
SENT_SOURCE = SENT_FACE + 24
SENT = SENT_SOURCE + 8
CHUNK = 8
KERNEL_WEIGHT = 0.02

VMEM = pl.BlockSpec(memory_space=pltpu.VMEM)
MIB = 1024 * 1024


def derivative_table():
    root = math.sqrt(3.0 / 7.0)
    points = [-1.0, -root, 0.0, root, 1.0]
    legendre = [(35.0 * x**4 - 30.0 * x**2 + 3.0) / 8.0 for x in points]
    table = np.zeros((5, 5))
    for row in range(5):
        for column in range(5):
            if row != column:
                table[row, column] = (
                    legendre[row] / legendre[column] / (points[row] - points[column])
                )
    table[0, 0] = -2.5
    table[4, 4] = 2.5
    return table


def cube_tables():
    deriv = derivative_table().astype(np.float32).astype(np.float64)
    line = np.array([0.1, 49.0 / 90.0, 32.0 / 45.0, 49.0 / 90.0, 0.1])
    cube = (line[:, None, None] * line[None, :, None] * line[None, None, :]).reshape(CUBE)
    cube = cube.astype(np.float32).astype(np.float64)
    along = [
        np.kron(np.eye(25), deriv),
        np.kron(np.eye(5), np.kron(deriv, np.eye(5))),
        np.kron(deriv, np.eye(25)),
    ]
    ahead = np.zeros((3 * LANES, LANES))
    back = np.zeros((3 * LANES, LANES))
    for i in range(3):
        ahead[i * LANES : i * LANES + CUBE, :CUBE] = along[i]
        back[i * LANES : i * LANES + CUBE, :CUBE] = -cube[:, None] * along[i]
    return (jnp.asarray(ahead, F32), jnp.asarray(back, F32))


def split(value):
    high = value.astype(BF16)
    return (high, (value - high.astype(F32)).astype(BF16))


def product(value, table, side):
    high, low = split(value)
    table_high, table_low = split(table)

    def dot(a, b):
        return lax.dot_general(a, b, (((1,), (side,)), ((), ())), preferred_element_type=F32)

    return dot(high, table_high) + (dot(low, table_high) + dot(high, table_low))


def pick(row, lanes):
    return jnp.take_along_axis(row, lanes, axis=1, mode="promise_in_bounds")


def gather_elements(wave_ref, index_ref, count):
    groups = []
    for t in range(0, ELEMS, 8):
        index = index_ref[t : t + 8, :]
        fine = index >> 7
        lane = index & 127
        found = [jnp.zeros((8, LANES), F32) for _ in range(count)]
        for c in range(FINE):
            hit = fine == c
            for r in range(count):
                row = wave_ref[r : r + 1, c * LANES : (c + 1) * LANES]
                found[r] = jnp.where(hit, pick(jnp.broadcast_to(row, (8, LANES)), lane), found[r])
        groups.append(found)
    return [jnp.concatenate(parts, 0) for parts in zip(*groups)]


def gather_faces(blocks, index_ref, targets):
    for face in range(2):
        for tile in range(3):
            at = FACE_ROW + 3 * face + tile
            index = jnp.broadcast_to(index_ref[at : at + 1, :], (8, LANES))
            fine = index >> 7
            lane = index & 127
            found = jnp.zeros((8, LANES), F32)
            for c in range(FINE):
                part = slice((c % 2) * LANES, (c % 2 + 1) * LANES)
                found = jnp.where(fine == c, pick(blocks[c // 2][:, part], lane), found)
            targets[face][SENT_FACE + 8 * tile : SENT_FACE + 8 * tile + 8, :] = found


def scatter(tiles, rows):
    step = lax.broadcasted_iota(jnp.int32, (16, LANES), 0)
    total = None
    for start in range(0, len(tiles), CHUNK):
        left = []
        right = []
        for tile, row in zip(tiles[start : start + CHUNK], rows[start : start + CHUNK]):
            index = jnp.broadcast_to(row, (16, LANES))
            coarse = (index >> 8).astype(F32).astype(BF16)
            offset = ((index & 255) - step).astype(F32).astype(BF16)
            high = tile.astype(BF16).astype(F32)
            pair = jnp.concatenate([high, tile - high], 0).astype(BF16)
            none = jnp.zeros_like(pair)
            one = jnp.ones_like(pair)
            left.append(jnp.concatenate([jnp.where(coarse == c, pair, none) for c in range(COARSE)], 0))
            right.append(jnp.concatenate([jnp.where(offset == c * 16, one, none) for c in range(16)], 0))
        part = lax.dot_general(
            jnp.concatenate(left, 1),
            jnp.concatenate(right, 1),
            (((1,), (1,)), ((), ())),
            preferred_element_type=F32,
        )
        total = part if total is None else total + part
    return [total[c * 16 : c * 16 + 8] + total[c * 16 + 8 : c * 16 + 16] for c in range(COARSE)]


def strains(fields, ahead):
    count = fields[0].shape[0]
    grads = product(jnp.concatenate(fields, 0), ahead, 1)

    def grad(f, i, j):
        r = (3 * f + j) * count
        return grads[r : r + count, i * LANES : (i + 1) * LANES]

    result = []
    for f in range(2):
        normal = [grad(f, i, i) for i in range(3)]
        dilation = normal[0] + normal[1] + normal[2]
        deviator = [n - dilation * (1.0 / 3.0) for n in normal]
        shear = {
            (i, j): 0.5 * (grad(f, i, j) + grad(f, j, i)) for i, j in ((0, 1), (0, 2), (1, 2))
        }
        result.append((dilation, deviator, shear))
    return result


def kernel_terms(strained, kappa, shear_mod):
    (dilation0, normal0, shear0), (dilation1, normal1, shear1) = strained
    bulk = -KERNEL_WEIGHT * kappa * dilation0 * dilation1
    inner = normal0[0] * normal1[0] + normal0[1] * normal1[1] + normal0[2] * normal1[2]
    cross = sum(shear0[key] * shear1[key] for key in shear0)
    return (bulk, -2.0 * KERNEL_WEIGHT * shear_mod * (inner + 2.0 * cross))


def element_forces(strained, kappa, shear_mod, back):
    twice = 2.0 * shear_mod
    columns = []
    for dilation, deviator, shear in strained:
        pressure = kappa * dilation
        for j in range(3):
            stress = [
                pressure + twice * deviator[j] if i == j else twice * shear[min(i, j), max(i, j)]
                for i in range(3)
            ]
            columns.append(jnp.concatenate(stress, 1))
    return product(jnp.concatenate(columns, 0), back, 0)


def element_tiles(tile_ref, forces, source_ref, step):
    count = forces.shape[0] // FIELDS
    tile_ref[...] = jnp.zeros_like(tile_ref)
    for r in range(FIELDS):
        tile_ref[pl.ds(r, count, stride=8), :] = forces[r * count : (r + 1) * count]
    for j in range(3):
        row = count * 8 + 3 + j
        tile_ref[row : row + 1, :] = source_ref[j, step : step + 1, :]
    return [tile_ref[8 * t : 8 * t + 8, :] for t in range(count + 1)]


def block(c):
    return slice(c * WIDE, (c + 1) * WIDE)


def even_partition():
    return lax.rem(lax.axis_index("mesh"), 2) == 0


def halves_in_order(value, even):
    first, second = value[:HALF], value[HALF:]
    return [jnp.where(even, second, first), jnp.where(even, first, second)]


def first_kernel(*refs):
    inputs, refs = refs[:14], refs[14:]
    wave, local, scale, index, to_inner, to_outer, totals = refs[:7]
    source, ahead, back = kept = refs[7:10]
    arrived = refs[10:21]
    before, tiles, sems = refs[21:]
    copies = [
        pltpu.make_async_copy(value, target, sems.at[i])
        for i, (value, target) in enumerate(zip(inputs, arrived + kept))
    ]
    for i in (2, 0, 1, 6, 7, 12, 13, 4, 5, 3, 11, 8, 9, 10):
        copies[i].start()
    forward, adjoint, connectivity, receivers, lower, upper, bulk_modulus, shear_modulus = arrived[:8]
    forward_prev, adjoint_prev, step_scale = arrived[8:]
    sent = (to_inner, to_outer)
    for ref in (wave, before, scale):
        ref[...] = jnp.zeros_like(ref)
    for ref in sent:
        ref[SENT_KAPPA:SENT_SLOTS, :] = jnp.zeros((2 * HALF, LANES), F32)
        ref[SENT_SOURCE:, :] = jnp.zeros((8, LANES), F32)
    index[0:FACE_ROW, :] = jnp.zeros((FACE_ROW, LANES), jnp.int32)
    index[FACE_ROW:, :] = jnp.full((8, LANES), -1, jnp.int32)
    for copy in copies[:8]:
        copy.wait()
    for j in range(3):
        wave[j : j + 1, 0:POINTS] = forward[j]
        wave[3 + j : 4 + j, 0:POINTS] = adjoint[j]
    even = even_partition()
    for face, (part, kappa, shear_mod) in enumerate(
        zip(*(halves_in_order(ref[...], even) for ref in (connectivity, bulk_modulus, shear_modulus)))
    ):
        index[face * HALF : (face + 1) * HALF, 0:CUBE] = part
        sent[face][SENT_KAPPA : SENT_KAPPA + HALF, 0:CUBE] = kappa
        sent[face][SENT_SHEAR : SENT_SHEAR + HALF, 0:CUBE] = shear_mod
    index[RECEIVER_ROW : RECEIVER_ROW + 1, :] = receivers[...]
    index[PARITY_ROW : PARITY_ROW + 1, :] = jnp.where(even, jnp.ones((1, LANES), jnp.int32), 0)
    faces = (jnp.where(even, upper[...], lower[...]), jnp.where(even, lower[...], upper[...]))
    for t in range(3):
        size = min(LANES, FACE - t * LANES)
        for face in range(2):
            at = FACE_ROW + 3 * face + t
            index[at : at + 1, 0:size] = faces[face][:, t * LANES : t * LANES + size]
    kappa = jnp.concatenate([ref[SENT_KAPPA : SENT_KAPPA + HALF, :] for ref in sent], 0)
    shear_mod = jnp.concatenate([ref[SENT_SHEAR : SENT_SHEAR + HALF, :] for ref in sent], 0)
    fields = gather_elements(wave, index, FIELDS)
    for copy in copies[8:]:
        copy.wait()
    for j in range(3):
        before[j : j + 1, 0:POINTS] = forward_prev[j]
        before[3 + j : 4 + j, 0:POINTS] = adjoint_prev[j]
    scale[0:1, 0:POINTS] = step_scale[...].reshape(1, POINTS)
    strained = strains(fields, ahead[...])
    bulk, shear = kernel_terms(strained, kappa, shear_mod)
    totals[0:ELEMS, :] = bulk
    totals[ELEMS : 2 * ELEMS, :] = shear
    forces = element_forces(strained, kappa, shear_mod, back[...])
    row = lax.broadcasted_iota(jnp.int32, (8, LANES), 0)
    lane = lax.broadcasted_iota(jnp.int32, (8, LANES), 1)
    marks = [
        jnp.where(row == SLOT_ROW, lane + (face * OUTER + t * LANES + 1), 0).astype(F32)
        for face in range(2)
        for t in range(3)
    ]
    values = element_tiles(tiles, forces, source, 0) + marks
    rows = [index[t : t + 1, :] for t in range(RECEIVER_ROW + 1)]
    rows += [index[FACE_ROW + t : FACE_ROW + t + 1, :] for t in range(6)]
    forces = scatter(values, rows)
    wide_row = lax.broadcasted_iota(jnp.int32, (8, WIDE), 0)
    at_faces = []
    for c in range(COARSE):
        factor = jnp.broadcast_to(scale[0:1, block(c)], (8, WIDE))
        local[:, block(c)] = jnp.where(
            wide_row == SLOT_ROW,
            forces[c],
            2.0 * wave[:, block(c)] - before[:, block(c)] + factor * forces[c],
        )
        at_faces.append(jnp.where(wide_row == SCALE_ROW, factor, forces[c]))
    gather_faces(at_faces, index, sent)
    receiver = jnp.broadcast_to(index[RECEIVER_ROW : RECEIVER_ROW + 1, :], (8, LANES))
    held = jnp.zeros((8, LANES), F32)
    for c in range(FINE):
        mark = local[SLOT_ROW : SLOT_ROW + 1, c * LANES : (c + 1) * LANES]
        got = pick(jnp.broadcast_to(mark, (8, LANES)), receiver & 127)
        held = jnp.where(receiver >> 7 == c, got, held)
    held = held[0:1]
    for face in range(2):
        for j in range(3):
            sent[face][SENT_SOURCE + j : SENT_SOURCE + j + 1, :] = source[j, 1:2, :]
        own = held < OUTER if face == 0 else held > OUTER
        sent[face][SENT_SOURCE + 3 : SENT_SOURCE + 4, :] = jnp.where(own, held - face * OUTER, 0.0)
    for r, value in enumerate(gather_elements(local, index, FIELDS + 1)):
        start = SENT_SLOTS if r == SLOT_ROW else r * HALF
        for face in range(2):
            part = value[face * HALF : (face + 1) * HALF]
            if r == SLOT_ROW and face:
                part = jnp.maximum(part - OUTER, 0.0)
            sent[face][start : start + HALF, :] = part


def slot_picks(ref):
    slots = ref[SENT_SLOTS : SENT_SLOTS + HALF, :].astype(jnp.int32) - 1
    return (slots >> 7, slots & 127)


def scaled_forces(own, other):
    added = []
    for t in range(3):
        at = SENT_FACE + 8 * t
        added.append(own[at + SCALE_ROW : at + SCALE_ROW + 1, :] * other[at : at + 8, :])
    return added


def completed(own, added):
    fine, lane = slot_picks(own)
    fields = []
    for r in range(FIELDS):
        value = own[r * HALF : (r + 1) * HALF, :]
        for t in range(3):
            got = pick(jnp.broadcast_to(added[t][r : r + 1, :], (HALF, LANES)), lane)
            value = value + jnp.where(fine == t, got, 0.0)
        fields.append(value)
    return fields


def both(first, second, start):
    return jnp.concatenate([ref[start : start + HALF, :] for ref in (first, second)], 0)


def second_kernel(added_inner, from_outer, to_inner, to_outer, earlier, ahead, index, terms, now, sums):
    inner = completed(to_inner, [added_inner[8 * t : 8 * t + 8, :] for t in range(3)])
    outer = completed(to_outer, scaled_forces(to_outer, from_outer))
    fields = [jnp.concatenate(pair, 0) for pair in zip(inner, outer)]
    for r in range(FIELDS):
        now[r * ELEMS : (r + 1) * ELEMS, :] = fields[r]
    kappa = both(to_inner, to_outer, SENT_KAPPA)
    shear_mod = both(to_inner, to_outer, SENT_SHEAR)
    found = kernel_terms(strains(fields, ahead[...]), kappa, shear_mod)
    even = jnp.broadcast_to(index[PARITY_ROW : PARITY_ROW + 1, :], (HALF, LANES)) == 1
    for which in range(2):
        start = which * ELEMS
        total = earlier[start : start + ELEMS, :] + found[which]
        sums[start : start + ELEMS, :] = jnp.concatenate(halves_in_order(total, even), 0)
    for which in range(2):
        for e in range(2):
            start = which * ELEMS + e
            for place, event in enumerate(ORDER[::4]):
                terms[4 * place : 4 * place + 4, 2 * which + e, :] = sums[
                    pl.ds(start + 2 * event, 4, stride=2), :
                ]


def third_kernel(
    from_inner,
    from_outer,
    to_inner,
    to_outer,
    now,
    wave,
    local,
    scale,
    index,
    source,
    ahead,
    back,
    forward,
    adjoint,
    result,
    tiles,
):
    halo = [
        completed(own, scaled_forces(own, other))
        for own, other in ((from_inner, to_inner), (from_outer, to_outer))
    ]
    fields = [
        jnp.concatenate([now[r * ELEMS : (r + 1) * ELEMS, :], halo[0][r], halo[1][r]], 0)
        for r in range(FIELDS)
    ]
    moduli = [
        jnp.concatenate([both(to_inner, to_outer, start), both(from_inner, from_outer, start)], 0)
        for start in (SENT_KAPPA, SENT_SHEAR)
    ]
    forces = element_forces(strains(fields, ahead[...]), *moduli, back[...])
    values = element_tiles(tiles, forces, source, 1)
    rows = [index[t : t + 1, :] for t in range(ELEMS)]
    faces = []
    for face, ref in enumerate((from_inner, from_outer)):
        fine, lane = slot_picks(ref)
        heard = ref[SENT_SOURCE + 3 : SENT_SOURCE + 4, :].astype(jnp.int32) - 1
        heard = jnp.broadcast_to(heard, (8, LANES))
        points = jnp.full((HALF, LANES), -1, jnp.int32)
        receivers = jnp.full((8, LANES), -1, jnp.int32)
        for t in range(3):
            at = FACE_ROW + 3 * face + t
            row = index[at : at + 1, :]
            points = jnp.where(fine == t, pick(jnp.broadcast_to(row, (HALF, LANES)), lane), points)
            got = pick(jnp.broadcast_to(row, (8, LANES)), heard & 127)
            receivers = jnp.where(heard >> 7 == t, got, receivers)
            values.append(2.0 * ref[SENT_FACE + 8 * t : SENT_FACE + 8 * t + 8, :])
            faces.append(row)
        rows += [points[t : t + 1, :] for t in range(HALF)]
        source_tile = ref[SENT_SOURCE : SENT_SOURCE + 8, :]
        values.append(jnp.concatenate([jnp.zeros((3, LANES), F32), source_tile[0:3], source_tile[4:6]], 0))
        faces.append(receivers[0:1])
    rows += [index[RECEIVER_ROW : RECEIVER_ROW + 1, :]] + faces
    added = scatter(values, rows)
    for c in range(COARSE):
        result[:, block(c)] = (
            2.0 * local[:, block(c)] - wave[:, block(c)] + scale[0:1, block(c)] * added[c]
        )
    for j in range(3):
        forward[j] = result[j : j + 1, 0:POINTS]
        adjoint[j] = result[3 + j : 4 + j, 0:POINTS]


def call(kernel, outs, scratch, args, place=VMEM):
    return pl.pallas_call(
        kernel,
        out_shape=[jax.ShapeDtypeStruct(shape, dtype) for shape, dtype in outs],
        in_specs=[place] * len(args),
        out_specs=[VMEM] * len(outs),
        scratch_shapes=scratch,
        compiler_params=pltpu.CompilerParams(vmem_limit_bytes=24 * MIB),
    )(*args)


def swap_faces(to_inner, to_outer):
    count = lax.axis_size("mesh")
    inner = [(i, i ^ 1) for i in range(count)]
    outer = [(i, i + 1 if i % 2 else i - 1) for i in range(1, count - 1)]
    return (lax.ppermute(to_inner, "mesh", inner), lax.ppermute(to_outer, "mesh", outer))


def shards(
    forward_now,
    forward_prev,
    adjoint_now,
    adjoint_prev,
    connectivity,
    lower_face,
    upper_face,
    bulk_modulus,
    shear_modulus,
    step_scale,
    receiver_points,
    adjoint_source,
):
    def rows(field):
        return field.transpose(1, 0, 2)

    padded = ((8, PADDED), F32)
    sent = ((SENT, LANES), F32)
    pair = ((2 * ELEMS, LANES), F32)
    inputs = [
        rows(forward_now),
        rows(adjoint_now),
        connectivity.T,
        receiver_points.reshape(1, LANES),
        lower_face,
        upper_face,
        bulk_modulus.T,
        shear_modulus.T,
        rows(forward_prev),
        rows(adjoint_prev),
        step_scale,
        adjoint_source[0].transpose(1, 0, 2),
        *cube_tables(),
    ]
    inputs = [pltpu.with_memory_space_constraint(value, pltpu.HBM) for value in inputs]
    wave, local, scale, index, to_inner, to_outer, earlier, source, ahead, back = call(
        first_kernel,
        [padded, padded, ((1, PADDED), F32), ((48, LANES), jnp.int32), sent, sent, pair]
        + [(value.shape, value.dtype) for value in inputs[11:]],
        [pltpu.VMEM(value.shape, value.dtype) for value in inputs[:11]]
        + [pltpu.VMEM(*padded)]
        + [pltpu.VMEM(((ELEMS + 1) * 8, LANES), F32)]
        + [pltpu.SemaphoreType.DMA((len(inputs),))],
        inputs,
        pl.BlockSpec(memory_space=pl.ANY),
    )
    from_inner, from_outer = swap_faces(to_inner, to_outer)
    added_inner = jnp.concatenate(scaled_forces(to_inner, from_inner), 0)
    terms, now = call(
        second_kernel,
        [((EVENTS, 4, LANES), F32), ((FIELDS * ELEMS, LANES), F32)],
        [pltpu.VMEM(*pair)],
        [added_inner, from_outer, to_inner, to_outer, earlier, ahead, index],
    )
    terms = lax.all_to_all(terms, "event", 0, 0, axis_index_groups=[ORDER], tiled=True)
    forward, adjoint = call(
        third_kernel,
        [((3, 1, POINTS), F32), ((3, 1, POINTS), F32)],
        [pltpu.VMEM(*padded), pltpu.VMEM(((2 * ELEMS + 1) * 8, LANES), F32)],
        [from_inner, from_outer, to_inner, to_outer, now, wave, local, scale, index, source, ahead, back],
    )
    kernels = jnp.sum(terms, axis=0)[:, :CUBE].reshape(2, 2, CUBE)
    return (rows(forward), rows(adjoint), kernels.transpose(0, 2, 1))


def solution(mesh):
    placed = (
        P("event", None, "mesh"),
        P("event", None, "mesh"),
        P("event", None, "mesh"),
        P("event", None, "mesh"),
        P(None, "mesh"),
        P("mesh", None),
        P("mesh", None),
        P(None, "mesh"),
        P(None, "mesh"),
        P("mesh"),
        P("mesh"),
        P("event", None, None, "mesh"),
    )
    return jax.shard_map(
        shards,
        mesh=mesh,
        in_specs=placed,
        out_specs=(
            P("event", None, "mesh"),
            P("event", None, "mesh"),
            P(None, None, ("mesh", "event")),
        ),
        check_vma=False,
    )
```

time: 45.9 us -> 41.7 us (0.908)
  the two profiles are of different devices: /device:TPU:34 before, /device:TPU:32 now
where the time goes in v3:
time: 41.7 us; the launch traced here: 41.4 us
  starting transfers between devices  27.6 us (66%)
  Pallas kernels  9.06 us (22%)
  waiting for transfers between devices  3.43 us (8%)
  between operations  0.67 us (2%)
  other arithmetic  0.61 us (1%)
    all_to_all x1, starting transfers between devices, shards(): lax.all_to_all(terms, 'event', 0, 0, axis_index_groups=[ORDER], tiled=True)  20.3 us
    pallas_call x3, Pallas kernels, call(): pl.pallas_call(kernel, out_shape=[jax.ShapeDtypeStruct(shape, dtype) for...  9.06 us
    ppermute x1, starting transfers between devices, swap_faces(): lax.ppermute(to_outer, 'mesh', outer)  5.42 us
    ppermute x1, starting transfers between devices, swap_faces(): lax.ppermute(to_inner, 'mesh', inner)  1.92 us
    all_to_all x1, waiting for transfers between devices, shards(): lax.all_to_all(terms, 'event', 0, 0, axis_index_groups=[ORDER], tiled=True)  1.37 us
    ppermute x1, waiting for transfers between devices, swap_faces(): lax.ppermute(to_inner, 'mesh', inner)  1.24 us
  transfers between devices with their start and end apart: 3, of which 3 were waited for; matrix products, arithmetic and copies ran while one was open for 0% of the time, Pallas kernels for 8%

profile of v3, /device:TPU:32, one launch (start us, length us, event | category | flops | bytes accessed | tf_op | source)
XLA Modules:
  0.0 41.4 jit_solution(3133632231339102922)
XLA Ops:
  0.6 4.5 %shard_map.157 = (f32[8,2816]{1,0:T(8,128)S(1)}, f32[8,2816]{1,0:T(8,128)S(1)}, f32[1,2816]{1,0:T(1,128)S(1)}, s32[48,128]{1,0:T(8,128)S(1)}, f32[176,128]{1,0:T...) custom-call(f32[3,1,2601]{2,1,0:T(1,128)} %bitcast.23, ...), custom_call_target="tpu_custom_call" | custom-call | tf_op jit(solution)/shard_map/pallas_call | solution.py:436
  5.1 5.4 %collective-permute-start.1 = (f32[176,128]{1,0:T(8,128)S(1)}, f32[176,128]{1,0:T(8,128)S(1)}, u32[]{:S(2)}, u32[]{:S(2)}) collective-permute-start(f32[176,128]{1,0:T(8,128)S(1)} %get-tuple-element.18.to_outer), channel_id=1, source_target_pairs={{16,32},{32,16},{48,64},{64,48},{80,96},{96,80},{112,128},{128,112... | collective-permute-start | bytes 270344 | tf_op jit(solution)/shard_map/ppermute | solution.py:450
  10.6 1.9 %collective-permute-start = (f32[176,128]{1,0:T(8,128)S(1)}, f32[176,128]{1,0:T(8,128)S(1)}, u32[]{:S(2)}, u32[]{:S(2)}) collective-permute-start(f32[176,128]{1,0:T(8,128)S(1)} %get-tuple-element.17.to_inner), channel_id=1, source_target_pairs={{0,16},{16,0},{32,48},{48,32},{64,80},{80,64},{96,112},{112,96},{1... | collective-permute-start | bytes 270344 | tf_op jit(solution)/shard_map/ppermute | solution.py:450
  12.5 1.2 %collective-permute-done.from_inner = f32[176,128]{1,0:T(8,128)S(1)} collective-permute-done((f32[176,128]{1,0:T(8,128)S(1)}, f32[176,128]{1,0:T(8,128)S(1)}, u32[]{:S(2)}, u32[]{:S(2)}) %collective-permute-start) | collective-permute-done | bytes 90144 | tf_op jit(solution)/shard_map/ppermute | solution.py:450
  13.8 0.8 %collective-permute-done.1.from_outer = f32[176,128]{1,0:T(8,128)S(1)} collective-permute-done((f32[176,128]{1,0:T(8,128)S(1)}, f32[176,128]{1,0:T(8,128)S(1)}, u32[]{:S(2)}, u32[]{:S(2)}) %collective-permute-start.1) | collective-permute-done | bytes 90144 | tf_op jit(solution)/shard_map/ppermute | solution.py:450
  14.6 1.1 %shard_map.158 = (f32[16,4,128]{2,1,0:T(4,128)}, f32[192,128]{1,0:T(8,128)S(1)}) custom-call(f32[24,128]{1,0:T(8,128)S(1)} %pad_maximum_fusion.added_inner, f32[176,128]{1,0:T(8,128)S(1)} %collective-permute-done.1.from_outer, f32[176,128]{1,0:T(8,128)S(1)} %get-tuple-element.17.to_inner, f32[176,128]{1,0:T(8,128)S(1)} %get-tuple-element.18.to_outer, ...), custom_call_target="tpu_custom_call" | custom-call | tf_op jit(solution)/shard_map/pallas_call | solution.py:436
  15.7 20.3 %all-to-all-start = ((f32[16,4,128]{2,1,0:T(4,128)}), f32[16,4,128]{2,1,0:T(4,128)S(1)}, u32[]{:S(2)}, u32[]{:S(2)}) async-start(f32[16,4,128]{2,1,0:T(4,128)} %get-tuple-element.30), calls=%async_computation | async-start | bytes 65536 | tf_op jit(solution)/shard_map/all_to_all | solution.py:508
  36.0 3.5 %shard_map.159 = (f32[3,1,2601]{2,1,0:T(1,128)}, f32[3,1,2601]{2,1,0:T(1,128)}) custom-call(f32[176,128]{1,0:T(8,128)S(1)} %collective-permute-done.from_inner, f32[176,128]{1,0:T(8,128)S(1)} %collective-permute-done.1.from_outer, f32[176,128]{1,0:T(8,128)S(1)} %get-tuple-element.17.to_inner, f32[176,128]{1,0:T(8,128)S(1)} %get-tuple-element.18.to_outer, ...), custom_call_target="tpu_custom_call" | custom-call | tf_op jit(solution)/shard_map/pallas_call | solution.py:436
  39.4 1.4 %all-to-all-done = f32[16,4,128]{2,1,0:T(4,128)S(1)} async-done(((f32[16,4,128]{2,1,0:T(4,128)}), f32[16,4,128]{2,1,0:T(4,128)S(1)}, u32[]{:S(2)}, u32[]{:S(2)}) %all-to-all-start) | async-done | bytes 32800 | tf_op jit(solution)/shard_map/all_to_all | solution.py:508
  40.8 0.6 %reduce_sum.9 = f32[4,128]{1,0:T(4,128)} reduce(f32[16,4,128]{2,1,0:T(4,128)S(1)} %all-to-all-done, f32[]{:T(128)} %constant.2.clone.1), dimensions={0}, to_apply=%region_0.0 | reduce | flops 7680 | bytes 34820 | tf_op jit(solution)/shard_map/reduce_sum | solution.py:515
  (3 shorter events, 0.0 us)
Async XLA Ops:
  5.1 9.4 %collective-permute-start.1 = (f32[176,128]{1,0:T(8,128)S(1)}, f32[176,128]{1,0:T(8,128)S(1)}, u32[]{:S(2)}, u32[]{:S(2)}) collective-permute-start(f32[176,128]{1,0:T(8,128)S(1)} %get-tuple-element.18.to_outer), channel_id=1, source_target_pairs={{16,32},{32,16},{48,64},{64,48},{80,96},{96,80},{112,128},{128,112... | collective-permute-start | bytes 270344 | tf_op jit(solution)/shard_map/ppermute | solution.py:450
  10.6 3.2 %collective-permute-start = (f32[176,128]{1,0:T(8,128)S(1)}, f32[176,128]{1,0:T(8,128)S(1)}, u32[]{:S(2)}, u32[]{:S(2)}) collective-permute-start(f32[176,128]{1,0:T(8,128)S(1)} %get-tuple-element.17.to_inner), channel_id=1, source_target_pairs={{0,16},{16,0},{32,48},{48,32},{64,80},{80,64},{96,112},{112,96},{1... | collective-permute-start | bytes 270344 | tf_op jit(solution)/shard_map/ppermute | solution.py:450
  15.7 25.1 %all-to-all-start = ((f32[16,4,128]{2,1,0:T(4,128)}), f32[16,4,128]{2,1,0:T(4,128)S(1)}, u32[]{:S(2)}, u32[]{:S(2)}) async-start(f32[16,4,128]{2,1,0:T(4,128)} %get-tuple-element.30), calls=%async_computation | async-start | bytes 65536 | tf_op jit(solution)/shard_map/all_to_all | solution.py:508

commit v4 on v3

--- a/solution.py
+++ b/solution.py
@@ -29,7 +29,7 @@
 SLOT_ROW = 6
 SCALE_ROW = 7
 OUTER = 512
-ORDER = [8, 9, 10, 11, 12, 13, 14, 15, 0, 1, 2, 3, 4, 5, 6, 7]
+ORDER = [10, 8, 9, 11, 12, 13, 14, 15, 0, 1, 2, 3, 4, 5, 6, 7]
 SENT_KAPPA = FIELDS * HALF
 SENT_SHEAR = SENT_KAPPA + HALF
 SENT_SLOTS = SENT_SHEAR + HALF
@@ -126,7 +126,8 @@
             targets[face][SENT_FACE + 8 * tile : SENT_FACE + 8 * tile + 8, :] = found
 
 
-def scatter(tiles, rows):
+def scatter(tiles, rows, blocks=COARSE, width=WIDE):
+    shift = width.bit_length() - 1
     step = lax.broadcasted_iota(jnp.int32, (16, LANES), 0)
     total = None
     for start in range(0, len(tiles), CHUNK):
@@ -134,14 +135,14 @@
         right = []
         for tile, row in zip(tiles[start : start + CHUNK], rows[start : start + CHUNK]):
             index = jnp.broadcast_to(row, (16, LANES))
-            coarse = (index >> 8).astype(F32).astype(BF16)
-            offset = ((index & 255) - step).astype(F32).astype(BF16)
+            coarse = (index >> shift).astype(F32).astype(BF16)
+            offset = ((index & (width - 1)) - step).astype(F32).astype(BF16)
             high = tile.astype(BF16).astype(F32)
             pair = jnp.concatenate([high, tile - high], 0).astype(BF16)
             none = jnp.zeros_like(pair)
             one = jnp.ones_like(pair)
-            left.append(jnp.concatenate([jnp.where(coarse == c, pair, none) for c in range(COARSE)], 0))
-            right.append(jnp.concatenate([jnp.where(offset == c * 16, one, none) for c in range(16)], 0))
+            left.append(jnp.concatenate([jnp.where(coarse == c, pair, none) for c in range(blocks)], 0))
+            right.append(jnp.concatenate([jnp.where(offset == c * 16, one, none) for c in range(width // 16)], 0))
         part = lax.dot_general(
             jnp.concatenate(left, 1),
             jnp.concatenate(right, 1),
@@ -149,7 +150,7 @@
             preferred_element_type=F32,
         )
         total = part if total is None else total + part
-    return [total[c * 16 : c * 16 + 8] + total[c * 16 + 8 : c * 16 + 16] for c in range(COARSE)]
+    return [total[c * 16 : c * 16 + 8] + total[c * 16 + 8 : c * 16 + 16] for c in range(blocks)]
 
 
 def strains(fields, ahead):
@@ -363,10 +364,9 @@
     for which in range(2):
         for e in range(2):
             start = which * ELEMS + e
-            for place, event in enumerate(ORDER[::4]):
-                terms[4 * place : 4 * place + 4, 2 * which + e, :] = sums[
-                    pl.ds(start + 2 * event, 4, stride=2), :
-                ]
+            for place, event in enumerate(ORDER):
+                row = start + 2 * event
+                terms[place, 2 * which + e : 2 * which + e + 1, :] = sums[row : row + 1, :]
 
 
 def third_kernel(
@@ -400,28 +400,26 @@
         for start in (SENT_KAPPA, SENT_SHEAR)
     ]
     forces = element_forces(strains(fields, ahead[...]), *moduli, back[...])
-    values = element_tiles(tiles, forces, source, 1)
-    rows = [index[t : t + 1, :] for t in range(ELEMS)]
-    faces = []
+    everything = element_tiles(tiles, forces, source, 1)
+    values = everything[:ELEMS] + everything[2 * ELEMS :]
+    rows = [index[t : t + 1, :] for t in range(RECEIVER_ROW + 1)]
     for face, ref in enumerate((from_inner, from_outer)):
-        fine, lane = slot_picks(ref)
+        start = ELEMS + face * HALF
+        slots = ref[SENT_SLOTS : SENT_SLOTS + HALF, :].astype(jnp.int32) - 1
+        held = scatter(everything[start : start + HALF], [slots[t : t + 1, :] for t in range(HALF)], 3, LANES)
         heard = ref[SENT_SOURCE + 3 : SENT_SOURCE + 4, :].astype(jnp.int32) - 1
         heard = jnp.broadcast_to(heard, (8, LANES))
-        points = jnp.full((HALF, LANES), -1, jnp.int32)
         receivers = jnp.full((8, LANES), -1, jnp.int32)
         for t in range(3):
             at = FACE_ROW + 3 * face + t
             row = index[at : at + 1, :]
-            points = jnp.where(fine == t, pick(jnp.broadcast_to(row, (HALF, LANES)), lane), points)
             got = pick(jnp.broadcast_to(row, (8, LANES)), heard & 127)
             receivers = jnp.where(heard >> 7 == t, got, receivers)
-            values.append(2.0 * ref[SENT_FACE + 8 * t : SENT_FACE + 8 * t + 8, :])
-            faces.append(row)
-        rows += [points[t : t + 1, :] for t in range(HALF)]
+            values.append(held[t] + 2.0 * ref[SENT_FACE + 8 * t : SENT_FACE + 8 * t + 8, :])
+            rows.append(row)
         source_tile = ref[SENT_SOURCE : SENT_SOURCE + 8, :]
         values.append(jnp.concatenate([jnp.zeros((3, LANES), F32), source_tile[0:3], source_tile[4:6]], 0))
-        faces.append(receivers[0:1])
-    rows += [index[RECEIVER_ROW : RECEIVER_ROW + 1, :]] + faces
+        rows.append(receivers[0:1])
     added = scatter(values, rows)
     for c in range(COARSE):
         result[:, block(c)] = (

time: 41.7 us -> 41 us (0.983)
  waiting for transfers between devices: 3.43 us -> 2.06 us
  starting transfers between devices: 27.6 us -> 28.3 us
    all_to_all x1, waiting for transfers between devices: 1.37 us -> 0.01 us  [shards(): lax.all_to_all(terms, 'event', 0, 0, axis_index_groups=[ORDER], tiled=True)]
    all_to_all x1, starting transfers between devices: 20.3 us -> 20.9 us  [shards(): lax.all_to_all(terms, 'event', 0, 0, axis_index_groups=[ORDER], tiled=True)]
  transfers between devices with their start and end apart: 3 -> 3, of which waited for: 3 -> 2; matrix products, arithmetic and copies ran while one was open for 0% -> 0% of each run, Pallas kernels for 8% -> 9%
where the time goes in v4:
time: 41 us; the launch traced here: 40.8 us
  starting transfers between devices  28.3 us (69%)
  Pallas kernels  9.16 us (22%)
  waiting for transfers between devices  2.06 us (5%)
  between operations  0.67 us (2%)
  other arithmetic  0.61 us (1%)
    all_to_all x1, starting transfers between devices, shards(): lax.all_to_all(terms, 'event', 0, 0, axis_index_groups=[ORDER], tiled=True)  20.9 us
    pallas_call x3, Pallas kernels, call(): pl.pallas_call(kernel, out_shape=[jax.ShapeDtypeStruct(shape, dtype) for...  9.16 us
    ppermute x1, starting transfers between devices, swap_faces(): lax.ppermute(to_outer, 'mesh', outer)  5.42 us
    ppermute x1, starting transfers between devices, swap_faces(): lax.ppermute(to_inner, 'mesh', inner)  1.92 us
    ppermute x1, waiting for transfers between devices, swap_faces(): lax.ppermute(to_inner, 'mesh', inner)  1.24 us
  transfers between devices with their start and end apart: 3, of which 2 were waited for; matrix products, arithmetic and copies ran while one was open for 0% of the time, Pallas kernels for 9%

profile of v4, /device:TPU:32, one launch (start us, length us, event | category | flops | bytes accessed | tf_op | source)
XLA Modules:
  0.0 40.8 jit_solution(6842171981319534981)
XLA Ops:
  0.6 4.5 %shard_map.157 = (f32[8,2816]{1,0:T(8,128)S(1)}, f32[8,2816]{1,0:T(8,128)S(1)}, f32[1,2816]{1,0:T(1,128)S(1)}, s32[48,128]{1,0:T(8,128)S(1)}, f32[176,128]{1,0:T...) custom-call(f32[3,1,2601]{2,1,0:T(1,128)} %bitcast.23, ...), custom_call_target="tpu_custom_call" | custom-call | tf_op jit(solution)/shard_map/pallas_call | solution.py:434
  5.1 5.4 %collective-permute-start.1 = (f32[176,128]{1,0:T(8,128)S(1)}, f32[176,128]{1,0:T(8,128)S(1)}, u32[]{:S(2)}, u32[]{:S(2)}) collective-permute-start(f32[176,128]{1,0:T(8,128)S(1)} %get-tuple-element.18.to_outer), channel_id=1, source_target_pairs={{16,32},{32,16},{48,64},{64,48},{80,96},{96,80},{112,128},{128,112... | collective-permute-start | bytes 270344 | tf_op jit(solution)/shard_map/ppermute | solution.py:448
  10.6 1.9 %collective-permute-start = (f32[176,128]{1,0:T(8,128)S(1)}, f32[176,128]{1,0:T(8,128)S(1)}, u32[]{:S(2)}, u32[]{:S(2)}) collective-permute-start(f32[176,128]{1,0:T(8,128)S(1)} %get-tuple-element.17.to_inner), channel_id=1, source_target_pairs={{0,16},{16,0},{32,48},{48,32},{64,80},{80,64},{96,112},{112,96},{1... | collective-permute-start | bytes 270344 | tf_op jit(solution)/shard_map/ppermute | solution.py:448
  12.5 1.2 %collective-permute-done.from_inner = f32[176,128]{1,0:T(8,128)S(1)} collective-permute-done((f32[176,128]{1,0:T(8,128)S(1)}, f32[176,128]{1,0:T(8,128)S(1)}, u32[]{:S(2)}, u32[]{:S(2)}) %collective-permute-start) | collective-permute-done | bytes 90144 | tf_op jit(solution)/shard_map/ppermute | solution.py:448
  13.8 0.8 %collective-permute-done.1.from_outer = f32[176,128]{1,0:T(8,128)S(1)} collective-permute-done((f32[176,128]{1,0:T(8,128)S(1)}, f32[176,128]{1,0:T(8,128)S(1)}, u32[]{:S(2)}, u32[]{:S(2)}) %collective-permute-start.1) | collective-permute-done | bytes 90144 | tf_op jit(solution)/shard_map/ppermute | solution.py:448
  14.6 1.1 %shard_map.158 = (f32[16,4,128]{2,1,0:T(4,128)}, f32[192,128]{1,0:T(8,128)S(1)}) custom-call(f32[24,128]{1,0:T(8,128)S(1)} %pad_maximum_fusion.added_inner, f32[176,128]{1,0:T(8,128)S(1)} %collective-permute-done.1.from_outer, f32[176,128]{1,0:T(8,128)S(1)} %get-tuple-element.17.to_inner, f32[176,128]{1,0:T(8,128)S(1)} %get-tuple-element.18.to_outer, ...), custom_call_target="tpu_custom_call" | custom-call | tf_op jit(solution)/shard_map/pallas_call | solution.py:434
  15.7 20.9 %all-to-all-start = ((f32[16,4,128]{2,1,0:T(4,128)}), f32[16,4,128]{2,1,0:T(4,128)S(1)}, u32[]{:S(2)}, u32[]{:S(2)}) async-start(f32[16,4,128]{2,1,0:T(4,128)} %get-tuple-element.30), calls=%async_computation | async-start | bytes 65536 | tf_op jit(solution)/shard_map/all_to_all | solution.py:506
  36.6 3.6 %shard_map.159 = (f32[3,1,2601]{2,1,0:T(1,128)}, f32[3,1,2601]{2,1,0:T(1,128)}) custom-call(f32[176,128]{1,0:T(8,128)S(1)} %collective-permute-done.from_inner, f32[176,128]{1,0:T(8,128)S(1)} %collective-permute-done.1.from_outer, f32[176,128]{1,0:T(8,128)S(1)} %get-tuple-element.17.to_inner, f32[176,128]{1,0:T(8,128)S(1)} %get-tuple-element.18.to_outer, ...), custom_call_target="tpu_custom_call" | custom-call | tf_op jit(solution)/shard_map/pallas_call | solution.py:434
  40.2 0.0 all-to-all-done
  40.2 0.6 %reduce_sum.9 = f32[4,128]{1,0:T(4,128)} reduce(f32[16,4,128]{2,1,0:T(4,128)S(1)} %all-to-all-done, f32[]{:T(128)} %constant.2.clone.1), dimensions={0}, to_apply=%region_0.0 | reduce | flops 7680 | bytes 34820 | tf_op jit(solution)/shard_map/reduce_sum | solution.py:513
  (3 shorter events, 0.0 us)
Async XLA Ops:
  5.1 9.4 %collective-permute-start.1 = (f32[176,128]{1,0:T(8,128)S(1)}, f32[176,128]{1,0:T(8,128)S(1)}, u32[]{:S(2)}, u32[]{:S(2)}) collective-permute-start(f32[176,128]{1,0:T(8,128)S(1)} %get-tuple-element.18.to_outer), channel_id=1, source_target_pairs={{16,32},{32,16},{48,64},{64,48},{80,96},{96,80},{112,128},{128,112... | collective-permute-start | bytes 270344 | tf_op jit(solution)/shard_map/ppermute | solution.py:448
  10.6 3.2 %collective-permute-start = (f32[176,128]{1,0:T(8,128)S(1)}, f32[176,128]{1,0:T(8,128)S(1)}, u32[]{:S(2)}, u32[]{:S(2)}) collective-permute-start(f32[176,128]{1,0:T(8,128)S(1)} %get-tuple-element.17.to_inner), channel_id=1, source_target_pairs={{0,16},{16,0},{32,48},{48,32},{64,80},{80,64},{96,112},{112,96},{1... | collective-permute-start | bytes 270344 | tf_op jit(solution)/shard_map/ppermute | solution.py:448
  15.7 24.5 %all-to-all-start = ((f32[16,4,128]{2,1,0:T(4,128)}), f32[16,4,128]{2,1,0:T(4,128)S(1)}, u32[]{:S(2)}, u32[]{:S(2)}) async-start(f32[16,4,128]{2,1,0:T(4,128)} %get-tuple-element.30), calls=%async_computation | async-start | bytes 65536 | tf_op jit(solution)/shard_map/all_to_all | solution.py:506
